TPU v7x, 256 devices: a whole 4x4x8 slice. The times are simulated.
256 devices in a mesh: dp: 8 (over y, x_hi), seq: 32 (over x_lo, z, core).
Axes of the slice: x: 4 (x_hi: 2, x_lo: 2; x = x_hi * 2 + x_lo), y: 4, z: 8, core: 2. Of those that a mesh axis runs over, the one named last changes fastest.
Arguments:
- query_lin: bfloat16 [32768, 4096], P(('dp', 'seq')), parts along dimension 0, may hold values from -6 to 6
- key_lin: bfloat16 [32768, 4096], P(('dp', 'seq')), parts along dimension 0, may hold values from -6 to 6
- value_lin: bfloat16 [32768, 4096], P(('dp', 'seq')), parts along dimension 0, may hold values from -100 to 100
- log_decay: bfloat16 [32768, 32], P(('dp', 'seq')), parts along dimension 0, may hold values from -2.2 to 0
- out_gate: bfloat16 [32768, 4096], P(('dp', 'seq')), parts along dimension 0, may hold values from -8 to 8
- norm_gain: float32 [4096], replicated, may hold values from 0.5 to 1.5
- state_in: float32 [256, 128, 128], P(('dp', 'seq')), parts along dimension 0, may hold values from -10 to 10
- query_soft: bfloat16 [32768, 4096], P(('dp', 'seq')), parts along dimension 0, may hold values from -4.5 to 4.5
- key_soft: bfloat16 [32768, 1024], P(('dp', 'seq')), parts along dimension 0, may hold values from -4.5 to 4.5
- value_soft: bfloat16 [32768, 1024], P(('dp', 'seq')), parts along dimension 0, may hold values from -6 to 6
Outputs:
- light_out: bfloat16 [32768, 4096], P(('dp', 'seq')), parts along dimension 0
- state_out: float32 [256, 128, 128], P(('dp', 'seq')), parts along dimension 0
- attn_out: bfloat16 [32768, 4096], P(('dp', 'seq')), parts along dimension 0
There are 8 independent parts, one for each index of `dp`. A program takes and returns all parts, laid end to end along the dimension named above; an argument that names none is the same for every part. Nothing has to cross between parts.
All inputs are finite; a program needn't handle non-finite values.
Results may differ from a plain program's by a relative error of at most 0.009.
Values may be sent and summed in bfloat16 or wider, within the bound.
A program may use at most 192 MiB of HBM per device.

v0:
```python
import math

import jax
import jax.numpy as jnp
from jax import lax
from jax.sharding import PartitionSpec as P

DH = 128
BLK = 128


norm_eps = 1e-06


def carried_in_2(x, axis, combine, identity):
    devices, index = (lax.axis_size(axis), lax.axis_index(axis))
    everything = jax.tree.map(lambda part: lax.all_gather(part, axis), x)
    start = jax.tree.map(
        lambda part, zero: jnp.broadcast_to(jnp.asarray(zero, part.dtype), part.shape), x, identity
    )

    def lap(k, before):
        reached = k < index
        new = combine(before, jax.tree.map(lambda part: part[k], everything))
        return jax.tree.map(lambda a, b: jnp.where(reached, a, b), new, before)

    return lax.fori_loop(0, devices, lap, start)


def spread_2(x, axis, root):
    mine = lax.axis_index(axis) == root
    return lax.psum(jnp.where(mine, x, jnp.zeros_like(x)), axis)


def lightning_blocks(queries, keys_act, values, decays, initial, block_len):
    row_count, head_count, head_width = queries.shape
    block_count = row_count // block_len
    shape_four = (block_count, block_len, head_count, head_width)
    query_blocks = queries.reshape(shape_four)
    key_blocks = keys_act.reshape(shape_four)
    value_blocks = values.reshape(shape_four)
    running = jnp.cumsum(decays.reshape(block_count, block_len, head_count), axis=1)
    closing = running[:, -1, :]
    scores = jnp.einsum(
        "bthd,bshd->bhts", query_blocks, key_blocks, preferred_element_type=jnp.float32
    )
    ordered = jnp.transpose(running, (0, 2, 1))
    spread = ordered[:, :, :, None] - ordered[:, :, None, :]
    causal = jnp.arange(block_len)[:, None] >= jnp.arange(block_len)[None, :]
    damping = jnp.where(causal, jnp.exp(jnp.where(causal, spread, 0.0)), 0.0)
    damped = (scores * damping).astype(jnp.bfloat16)
    inner = jnp.einsum("bhts,bshd->bthd", damped, value_blocks, preferred_element_type=jnp.float32)
    key_decayed = (
        key_blocks.astype(jnp.float32) * jnp.exp(closing[:, None, :] - running)[..., None]
    ).astype(jnp.bfloat16)
    block_states = jnp.einsum(
        "bshd,bshe->bhde", key_decayed, value_blocks, preferred_element_type=jnp.float32
    )
    query_decayed = query_blocks.astype(jnp.float32) * jnp.exp(running)[..., None]
    block_decay = jnp.exp(closing)

    def advance(carried_state, block_items):
        query_part, state_part, decay_part = block_items
        reached = jnp.einsum(
            "thd,hde->the", query_part, carried_state, precision=lax.Precision.HIGHEST
        )
        return (decay_part[:, None, None] * carried_state + state_part, reached)

    final_state, reached = lax.scan(advance, initial, (query_decayed, block_states, block_decay))
    return ((inner + reached).reshape(row_count, head_count, head_width), final_state)


def finish_rows(mixed_rows, out_gate, norm_gain):
    mean_square = jnp.mean(mixed_rows * mixed_rows, axis=1, keepdims=True)
    normed = mixed_rows * lax.rsqrt(mean_square + norm_eps)
    gated = normed * norm_gain * jax.nn.sigmoid(out_gate.astype(jnp.float32))
    return gated.astype(jnp.bfloat16)


def masked_softmax(scores, causal):
    masked = jnp.where(causal, scores, -jnp.inf)
    row_max = jnp.max(masked, axis=-1, keepdims=True)
    raised = jnp.exp(masked - row_max)
    row_total = jnp.sum(raised, axis=-1, keepdims=True)
    return (raised.astype(jnp.bfloat16), row_total)


def activate(query_rows, key_rows, value_rows, row_count, head_count):
    queries = (
        jax.nn.silu(query_rows.astype(jnp.float32))
        .astype(jnp.bfloat16)
        .reshape(row_count, head_count, DH)
    )
    keys_act = (
        (jax.nn.silu(key_rows.astype(jnp.float32)) * DH ** (-0.5))
        .astype(jnp.bfloat16)
        .reshape(row_count, head_count, DH)
    )
    values = value_rows.reshape(row_count, head_count, DH)
    return (queries, keys_act, values)


def chain_step(earlier, later):
    return (earlier[0] * later[0], later[0][:, None, None] * earlier[1] + later[1])


def shards(
    query_lin,
    key_lin,
    value_lin,
    log_decay,
    out_gate,
    norm_gain,
    state_in,
    query_soft,
    key_soft,
    value_soft,
):
    seq_size = lax.axis_size("seq")
    tok_rows = query_lin.shape[0]
    lin_width = query_lin.shape[1]
    lin_heads = lin_width // DH
    kv_heads = key_soft.shape[1] // DH
    copies = seq_size // kv_heads
    own_heads = lin_heads // seq_size

    def spread_heads(array):
        widened = jnp.repeat(array.reshape(tok_rows, kv_heads, DH), copies, axis=1)
        return widened.reshape(tok_rows, seq_size * DH)

    query_heads, key_heads, value_heads = (
        lax.all_to_all(query_soft, "seq", split_axis=1, concat_axis=0, tiled=True),
        lax.all_to_all(spread_heads(key_soft), "seq", split_axis=1, concat_axis=0, tiled=True),
        lax.all_to_all(spread_heads(value_soft), "seq", split_axis=1, concat_axis=0, tiled=True),
    )
    queries, keys_act, values = activate(query_lin, key_lin, value_lin, tok_rows, lin_heads)
    decays = log_decay.astype(jnp.float32)
    empty_state = jnp.zeros((lin_heads, DH, DH), jnp.float32)
    mixed_local, state_local = lightning_blocks(queries, keys_act, values, decays, empty_state, BLK)
    decay_total = jnp.exp(jnp.sum(decays, axis=0))
    identity = (jnp.ones((lin_heads,), jnp.float32), jnp.zeros((lin_heads, DH, DH), jnp.float32))
    before_decay, before_state = carried_in_2(
        (decay_total, state_local), "seq", chain_step, identity
    )
    full_start = lax.all_gather(state_in, "seq", axis=0, tiled=True)
    entering = before_decay[:, None, None] * full_start + before_state
    running = jnp.exp(jnp.cumsum(decays, axis=0))
    carried_in = jnp.einsum(
        "thd,hde->the",
        queries.astype(jnp.float32) * running[:, :, None],
        entering,
        precision=lax.Precision.HIGHEST,
    )
    mixed_rows = (mixed_local + carried_in).reshape(tok_rows, lin_width)
    leaving = decay_total[:, None, None] * entering + state_local
    whole_end = spread_2(leaving, "seq", seq_size - 1)
    state_out = lax.dynamic_slice_in_dim(whole_end, lax.axis_index("seq") * own_heads, own_heads, 0)
    light_out = finish_rows(mixed_rows, out_gate, norm_gain)
    total_rows = query_heads.shape[0]
    head_share = query_heads.shape[1] // DH
    query_groups = query_heads.reshape(total_rows, head_share, DH)
    block_rows = math.gcd(total_rows, 512)
    score_scale = DH ** (-0.5)
    pieces = []
    for offset in range(0, total_rows, block_rows):
        stop_row = offset + block_rows
        scores = (
            jnp.einsum(
                "thd,sd->hts",
                query_groups[offset:stop_row],
                key_heads[:stop_row],
                preferred_element_type=jnp.float32,
            )
            * score_scale
        )
        causal = (offset + jnp.arange(block_rows))[:, None] >= jnp.arange(stop_row)[None, :]
        raised, row_total = masked_softmax(scores, causal[None, :, :])
        summed = jnp.einsum(
            "hts,sd->thd", raised, value_heads[:stop_row], preferred_element_type=jnp.float32
        )
        result = (summed / jnp.transpose(row_total, (1, 0, 2))).astype(jnp.bfloat16)
        pieces.append(result.reshape(block_rows, head_share * DH))
    attn_heads = jnp.concatenate(pieces, axis=0)
    attn_out = lax.all_to_all(attn_heads, "seq", split_axis=0, concat_axis=1, tiled=True)
    return (light_out, state_out, attn_out)


def solution(mesh):
    return jax.shard_map(
        shards,
        mesh=mesh,
        in_specs=(
            P(("dp", "seq"), None),
            P(("dp", "seq"), None),
            P(("dp", "seq"), None),
            P(("dp", "seq"), None),
            P(("dp", "seq"), None),
            P(),
            P(("dp", "seq"), None, None),
            P(("dp", "seq"), None),
            P(("dp", "seq"), None),
            P(("dp", "seq"), None),
        ),
        out_specs=(P(("dp", "seq"), None), P(("dp", "seq"), None, None), P(("dp", "seq"), None)),
        check_vma=False,
    )
```

profile of v0, /device:TPU:1, one launch (start us, length us, event | category | flops | bytes accessed | tf_op | source)
XLA Modules:
  0.0 767.7 jit_solution(7476002560801590012)
XLA Ops:
  15.0 11.1 %all-to-all-start.2 = ((bf16[128,32,128]{2,0,1:T(8,128)(2,1)}), bf16[128,32,128]{2,0,1:T(8,128)(2,1)S(1)}, u32[]{:S(2)}, u32[]{:S(2)}) async-start(bf16[128,32,128]{2,0,1:T(8,128)(2,1)} %bitcast.25), calls=%async_computation.2 | async-start | bytes 2097152 | tf_op jit(solution)/shard_map/all_to_all | solution.py:134
  26.1 36.9 %all-to-all-done.2 = bf16[128,32,128]{2,0,1:T(8,128)(2,1)S(1)} async-done(((bf16[128,32,128]{2,0,1:T(8,128)(2,1)}), bf16[128,32,128]{2,0,1:T(8,128)(2,1)S(1)}, u32[]{:S(2)}, u32[]{:S(2)}) %all-to-all-start.2) | async-done | bytes 1048608 | tf_op jit(solution)/shard_map/all_to_all | solution.py:134
  64.3 6.4 all-to-all-start
  71.4 2.3 copy.117
  75.1 33.3 %all-to-all-done = bf16[128,32,128]{2,0,1:T(8,128)(2,1)S(1)} async-done(((bf16[128,32,128]{2,0,1:T(8,128)(2,1)}), bf16[128,32,128]{2,0,1:T(8,128)(2,1)S(1)}, u32[]{:S(2)}, u32[]{:S(2)}) %all-to-all-start) | async-done | bytes 1048608 | tf_op jit(solution)/shard_map/all_to_all | solution.py:133
  108.3 6.4 all-to-all-start.1
  116.4 81.9 %all-reduce = f32[1024]{0:T(1024)S(1)} all-reduce(f32[1024]{0:T(1024)S(1)} %get-tuple-element.179), channel_id=2, replica_groups=mesh['dp'=8,'seq'=32] {'seq'}, use_global_device_ids=true, to_apply=%add | all-reduce | flops 1024 | bytes 8192
  202.6 7.5 fusion.40
  210.0 4.4 fusion.54
  231.0 2.1 fusion.187
  260.7 2.8 fusion.150
  272.2 2.2 fusion.114
  274.4 5.6 all-to-all-start.3
  280.1 178.7 %all-gather.7.cloned.1.call-done = f32[1024,128,128]{2,1,0:T(8,128)} async-done(((f32[32,128,128]{2,1,0:T(8,128)}), f32[1024,128,128]{2,1,0:T(8,128)}) %all-gather.7.cloned.1.call-update) | async-done | bytes 67108880 | tf_op jit(solution)/shard_map/all_gather | solution.py:17
  458.8 68.7 %while.10 = (s32[]{:T(128)}, f32[32]{0:T(128)S(1)}, f32[32,128,128]{2,1,0:T(8,128)S(1)}, s32[]{:T(128)}, f32[32,32]{1,0:T(8,128)S(1)}, /*index=5*/f32[32,32,128,128]{3,2,1,0:T(8,128)}, s32[]{:T(128)}, s32[]{:T(128)}) while((s32[]{:T(128)}, f32[32]{0:T(128)S(1)}, f32[32,128,128]{2,1,0:T(8,128)S(1)}, s32[]{:T(128)}, ...), condition=%wide.region_3.4_spmd.clone, body=%wide.region_2.3_spmd.clone.sunk | while | flops 2097252 | bytes 6292219 | solution.py:27
  461.0 2.1 fusion.235
  463.1 2.1 fusion.235
  465.2 2.1 fusion.235
  467.4 2.1 fusion.235
  469.5 2.1 fusion.235
  471.7 2.1 fusion.235
  473.8 2.1 fusion.235
  476.0 2.1 fusion.235
  478.1 2.1 fusion.235
  480.3 2.1 fusion.235
  482.4 2.1 fusion.235
  484.6 2.1 fusion.235
  486.7 2.1 fusion.235
  488.9 2.1 fusion.235
  491.0 2.1 fusion.235
  493.1 2.1 fusion.235
  495.3 2.1 fusion.235
  497.4 2.1 fusion.235
  499.6 2.1 fusion.235
  501.7 2.1 fusion.235
  503.9 2.1 fusion.235
  506.1 2.1 fusion.235
  508.2 2.1 fusion.235
  510.4 2.1 fusion.235
  512.5 2.1 fusion.235
  514.7 2.1 fusion.235
  516.8 2.1 fusion.235
  523.2 2.1 fusion.235
  525.4 2.1 fusion.235
  527.5 4.0 add_select_fusion
  533.5 8.2 %multiply_reduce_fusion = (f32[128]{0:T(128)S(1)}, f32[128,32,128]{0,2,1:T(8,128)}) fusion(f32[128,32]{0,1:T(8,128)S(1)} %copy-done.34, f32[32,128,128]{2,1,0:T(8,128)S(1)} %get-tuple-element.132, f32[32,128,128]{2,1,0:T(8,128)S(1)} %copy-done.12, f32[32]{0:T(128)S(1)} %get-tuple-element.131, f32[32,128,128]{2,1,0:T(8,128)} %fusion.40, ...), kind=kOutput, calls=%fused_computation.77 | convolution fusion | flops 812646272 | bytes 11551360 | tf_op jit(solution)/shard_map/thd,hde->the/dot_general | solution.py:148
  543.7 2.9 multiply_convert_fusion
  546.6 212.9 %all-reduce.3.cloned.1.call-done = f32[32,128,128]{2,1,0:T(8,128)} async-done(((f32[32,128,128]{2,1,0:T(8,128)}), f32[32,128,128]{2,1,0:T(8,128)}) %all-reduce.3.cloned.1.call-update) | async-done | bytes 2097168 | tf_op jit(solution)/shard_map/psum | solution.py:32
  (219 shorter events, 81.3 us)
Async XLA Ops:
  7.2 3.8 copy-start
  7.2 451.6 %all-gather.7.cloned.1.call-start = ((), (), s32[]{:S(2)}) async-start(), calls=%async_computation.6 | async-start | bytes 69206016 | tf_op jit(solution)/shard_map/all_gather | solution.py:17
  10.9 1.9 copy-start.8
  13.7 12.3 %copy-start.22 = (bf16[128,1024]{1,0:T(8,128)(2,1)S(1)}, bf16[128,1024]{1,0:T(8,128)(2,1)}, u32[]{:S(2)}) copy-start(bf16[128,1024]{1,0:T(8,128)(2,1)} %param.20) | copy-start | bytes 786436
  15.0 48.0 %all-to-all-start.2 = ((bf16[128,32,128]{2,0,1:T(8,128)(2,1)}), bf16[128,32,128]{2,0,1:T(8,128)(2,1)S(1)}, u32[]{:S(2)}, u32[]{:S(2)}) async-start(bf16[128,32,128]{2,0,1:T(8,128)(2,1)} %bitcast.25), calls=%async_computation.2 | async-start | bytes 2097152 | tf_op jit(solution)/shard_map/all_to_all | solution.py:134
  62.9 10.7 %copy-start.2 = (bf16[128,32,128]{2,0,1:T(8,128)(2,1)}, bf16[128,32,128]{2,0,1:T(8,128)(2,1)S(1)}, u32[]{:S(2)}) copy-start(bf16[128,32,128]{2,0,1:T(8,128)(2,1)S(1)} %all-to-all-done.2) | copy-start | bytes 3145732
  64.3 9.4 %copy-start.43 = (u32[256]{0:T(256)S(1)}, u32[256]{0:T(256)}, u32[]{:S(2)}) copy-start(u32[256]{0:T(256)} %constant.102) | copy-start | bytes 3076
  64.3 10.7 %copy-start.31 = (bf16[128,32]{0,1:T(8,128)(2,1)S(1)}, bf16[128,32]{0,1:T(8,128)(2,1)}, u32[]{:S(2)}) copy-start(bf16[128,32]{0,1:T(8,128)(2,1)} %param.15) | copy-start | bytes 24580
  64.3 44.0 %all-to-all-start = ((bf16[128,32,128]{2,0,1:T(8,128)(2,1)}), bf16[128,32,128]{2,0,1:T(8,128)(2,1)S(1)}, u32[]{:S(2)}, u32[]{:S(2)}) async-start(bf16[128,32,128]{2,0,1:T(8,128)(2,1)} %bitcast.440), calls=%async_computation | async-start | bytes 2097152 | tf_op jit(solution)/shard_map/all_to_all | solution.py:133
  70.6 456.9 %all-gather.5.cloned.1.call-start = ((), (), s32[]{:S(2)}) async-start(), calls=%async_computation.4 | async-start | bytes 2162688 | tf_op jit(solution)/shard_map/all_gather | solution.py:145
  108.3 7.1 copy-start.5
  108.3 122.7 %all-to-all-start.1 = ((bf16[128,32,128]{0,2,1:T(8,128)(2,1)}), bf16[128,32,128]{0,2,1:T(8,128)(2,1)}, u32[]{:S(2)}, u32[]{:S(2)}) async-start(bf16[128,32,128]{0,2,1:T(8,128)(2,1)} %bitcast.441), calls=%async_computation.1 | async-start | bytes 2097152 | tf_op jit(solution)/shard_map/all_to_all | solution.py:132
  214.4 8.5 %copy-start.6 = (bf16[128,32,128]{2,0,1:T(8,128)(2,1)S(1)}, bf16[128,32,128]{2,0,1:T(8,128)(2,1)}, u32[]{:S(2)}) copy-start(bf16[128,32,128]{2,0,1:T(8,128)(2,1)} %copy-done.5) | copy-start | bytes 3145732
  214.4 9.2 %copy-start.3 = (bf16[128,32,128]{2,0,1:T(8,128)(2,1)S(1)}, bf16[128,32,128]{2,0,1:T(8,128)(2,1)}, u32[]{:S(2)}) copy-start(bf16[128,32,128]{2,0,1:T(8,128)(2,1)} %copy-done.2) | copy-start | bytes 3145732
  242.5 1.6 copy-start.26
  242.5 2.6 copy-start.24
  242.5 2.6 copy-start.30
  242.5 2.6 copy-start.42
  245.6 1.3 copy-start.13
  246.9 1.1 copy-start.28
  246.9 1.1 copy-start.40
  248.7 1.2 copy-start.17
  248.7 1.2 copy-start.27
  248.7 1.2 copy-start.39
  250.8 1.2 copy-start.16
  250.8 1.2 copy-start.25
  250.9 1.1 copy-start.38
  253.0 2.7 copy-start.4
  253.1 2.7 copy-start.15
  253.1 2.7 copy-start.37
  256.9 1.2 copy-start.7
  256.9 1.2 copy-start.36
  259.5 1.2 copy-start.23
  260.7 2.9 copy-start.19
  263.6 1.3 copy-start.14
  264.9 1.4 copy-start.11
  264.9 3.0 slice-start
  266.3 2.2 slice-start.1
  266.3 2.4 copy-start.10
  268.7 1.7 copy-start.9
  274.4 184.4 %copy-start.32 = (f32[32]{0:T(128)S(1)}, f32[32]{0:T(128)}, u32[]{:S(2)}) copy-start(f32[32]{0:T(128)} %custom-call) | copy-start | bytes 388
  274.4 257.1 %all-to-all-start.3 = ((bf16[32,128,128]{2,1,0:T(8,128)(2,1)}), bf16[32,128,128]{2,1,0:T(8,128)(2,1)S(1)}, u32[]{:S(2)}, u32[]{:S(2)}) async-start(bf16[32,128,128]{2,1,0:T(8,128)(2,1)} %bitcast.447), calls=%async_computation.3 | async-start | bytes 2097152 | tf_op jit(solution)/shard_map/all_to_all | solution.py:184
  280.1 479.4 %all-reduce.3.cloned.1.call-start = ((), (), s32[]{:S(2)}) async-start(), calls=%async_computation.5 | async-start | bytes 4194304 | tf_op jit(solution)/shard_map/psum | solution.py:32
  458.8 68.7 %copy-start.35 = (f32[32]{0:T(128)S(1)}, f32[32]{0:T(128)}, u32[]{:S(2)}) copy-start(f32[32]{0:T(128)} %get-tuple-element.178) | copy-start | bytes 388
  531.5 1.2 copy-start.34
  531.6 2.0 copy-start.12
  541.7 2.0 copy-start.33
  543.7 217.3 %copy-start.1 = (bf16[128,4096]{1,0:T(8,128)(2,1)S(1)}, bf16[128,4096]{1,0:T(8,128)(2,1)}, u32[]{:S(2)}) copy-start(bf16[128,4096]{1,0:T(8,128)(2,1)} %param.14) | copy-start | bytes 3145732
  (5 other events, 5.0 us)
Sparse Core Ops, SparseCore 0:
  12.9 445.8 all-gather.6
  460.7 64.7 all-gather.4
  531.7 227.7 all-reduce.2
where the time goes:
time: 774 us; the launch traced here: 768 us
  waiting for transfers between devices  462 us (60%)
  other arithmetic  87.7 us (11%)
  blocking collectives  81.9 us (11%)
  local copies, waits for them, and re-layouts  46.8 us (6%)
  matrix products  43.3 us (6%)
  starting transfers between devices  29.5 us (4%)
  between operations  15.1 us (2%)
    psum x1, waiting for transfers between devices, spread_2(): return lax.psum(jnp.where(mine, x, jnp.zeros_like(x)), axis)  213 us
    all_gather x1, waiting for transfers between devices, carried_in_2(): everything = jax.tree.map(lambda part: lax.all_gather(part, axis), x)  179 us
    unnamed x1, blocking collectives  81.9 us
    select_n x64, other arithmetic, lap(): return jax.tree.map(lambda a, b: jnp.where(reached, a, b), new, before)  67.8 us
    all_to_all x1, waiting for transfers between devices, shards(): lax.all_to_all(spread_heads(value_soft), 'seq', split_axis=1, concat_axis...  36.9 us
    all_to_all x1, waiting for transfers between devices, shards(): lax.all_to_all(spread_heads(key_soft), 'seq', split_axis=1, concat_axis=0...  33.3 us
  transfers between devices with their start and end apart: 7, of which 4 were waited for; matrix products, arithmetic and copies ran while one was open for 21% of the time, Pallas kernels for 0%

commit v1 on v0

v1 whole, which is shorter than its diff:
```python
import functools
import math

import jax
import jax.numpy as jnp
from jax import lax
from jax.experimental import pallas as pl
from jax.experimental.pallas import tpu as pltpu
from jax.sharding import PartitionSpec as P

DH = 128
NZ = 8
LHEADS = 32
NORM_EPS = 1e-6
SCALE = DH ** (-0.5)
EXP2_SCALE = SCALE * math.log2(math.e)
MASKED = -1e30
MESH = pl.DeviceIdType.MESH
F32 = jnp.float32
BF16 = jnp.bfloat16
ROWS_BY_ROWS = (((1,), (1,)), ((), ()))
COLS_BY_COLS = (((0,), (0,)), ((), ()))
Z_ORDER = (4, 3, 5, 2, 6, 1, 7)


def place(x, z, c):
    return (x * NZ + z) * 2 + c


def block(index):
    return pl.ds(pl.multiple_of(index * DH, DH), DH)


def wide(index, width):
    return pl.ds(pl.multiple_of(index * width, width), width)


def kernel(
    ql_in, kl_in, vl_in, ld_in, gate_in, gain_in, state_in, q_in, k_in, v_in,
    light_out, state_out, attn_out,
    kv, qx, qs, acc, top, low, ob,
    qlv, klv, vlv, gtv, lin, ct, cv, s_own, s_oth, s_par, ssend, sgot, eout, egot, ent, esend,
    stin, t0, fin, dt, chd, sq,
    lsem, kvs, kvr, qsend, qrecv, st_s, st_r, d_s, d_r, sp_s, sp_r, cd_s, cd_r, sa_s, sa_r,
    eo_s, eo_r, t_s, t_r, so_s, so_r, ep_s, ep_r, ag_s, ag_r, o_s, o_r, out_s,
):
    me = lax.axis_index("seq")
    x = me // (2 * NZ)
    z = (me // 2) % NZ
    c = me % 2
    quad = x * 2 + c
    mates = {1: (x, 1 - c), 2: (1 - x, c), 3: (1 - x, 1 - c)}

    def mate_quad(p):
        mx, mc = mates[p]
        return mx * 2 + mc

    def mate_at(p):
        mx, mc = mates[p]
        return place(mx, z, mc)

    def up(k):
        return (z + k) % NZ

    def remote(src, dst, send, recv, to):
        return pltpu.make_async_remote_copy(
            src_ref=src, dst_ref=dst, send_sem=send, recv_sem=recv,
            device_id={"seq": to}, device_id_type=MESH,
        )

    sends = []

    def go(copy):
        copy.start()
        sends.append(copy)

    barrier = pltpu.get_barrier_semaphore()
    peers = [mate_at(p) for p in (1, 2, 3)] + [place(x, up(k), c) for k in range(1, NZ)]
    for peer in peers:
        pl.semaphore_signal(barrier, inc=1, device_id={"seq": peer}, device_id_type=MESH)

    loads = [
        pltpu.make_async_copy(kl_in, klv, lsem.at[0]),
        pltpu.make_async_copy(vl_in, vlv, lsem.at[1]),
        pltpu.make_async_copy(ql_in, qlv, lsem.at[2]),
        pltpu.make_async_copy(gate_in, gtv, lsem.at[3]),
    ]
    for load in loads:
        load.start()

    def head_of(n, parity):
        return 16 * (n % 2) + 2 * (n // 2) + parity

    t_row = lax.broadcasted_iota(jnp.int32, (DH, DH), 0)
    t_col = lax.broadcasted_iota(jnp.int32, (DH, DH), 1)
    tril = jnp.where(t_row >= t_col, 1.0, 0.0).astype(BF16)
    cum = jnp.dot(tril, ld_in[...], preferred_element_type=F32)
    cv[...] = cum
    cum_t = jnp.transpose(cum)
    ct[...] = cum_t
    dt[c] = jnp.broadcast_to(cum_t[:, DH - 1 :], (LHEADS, DH))

    pl.semaphore_wait(barrier, len(peers))

    def kv_quad(hh, sel, p):
        src_all = (k_in, v_in)[sel]
        head = mate_quad(p) * 2 + hh
        return remote(
            src_all.at[:, block(head)], kv.at[z, hh, sel, block(quad), :],
            kvs.at[hh, sel, p], kvr.at[hh, sel, p], mate_at(p),
        )

    def kv_own(hh, sel):
        src_all = (k_in, v_in)[sel]
        return pltpu.make_async_copy(
            src_all.at[:, block(quad * 2 + hh)], kv.at[z, hh, sel, block(quad), :], kvr.at[hh, sel, 0]
        )

    def q_quad(p):
        return remote(
            q_in.at[:, wide(mate_quad(p), 1024)], qx.at[quad], qsend.at[p], qrecv.at[p], mate_at(p)
        )

    q_own = pltpu.make_async_copy(q_in.at[:, wide(quad, 1024)], qx.at[quad], qrecv.at[0])
    for hh in range(2):
        for p in (2, 3, 1):
            for sel in range(2):
                go(kv_quad(hh, sel, p))
        for sel in range(2):
            kv_own(hh, sel).start()
    go(remote(dt.at[c], dt.at[c], d_s, d_r, mate_at(1)))

    st_own = pltpu.make_async_copy(state_in.at[0], stin.at[0], st_r.at[0])
    st_move = remote(state_in.at[0], stin.at[1], st_s, st_r.at[1], mate_at(2))

    @pl.when(x == 0)
    def _():
        st_own.start()

    @pl.when(x == 1)
    def _():
        st_move.start()

    for p in (2, 3, 1):
        go(q_quad(p))
    q_own.start()

    def column(h):
        lanes = lax.broadcasted_iota(jnp.int32, (DH, LHEADS), 1)
        return jnp.sum(jnp.where(lanes == h, cv[...], 0.0), axis=1, keepdims=True)

    def silu(u):
        return u / (1.0 + jnp.exp(-u))

    def block_states(parity, target):
        def step(n, carry):
            h = head_of(n, parity)
            keys = (silu(klv[:, block(h)].astype(F32)) * SCALE).astype(BF16)
            klv[:, block(h)] = keys
            col = column(h)
            decayed = (keys.astype(F32) * jnp.exp(col[DH - 1 :, :] - col)).astype(BF16)
            state = lax.dot_general(
                decayed, vlv[:, block(h)], COLS_BY_COLS, preferred_element_type=F32
            )
            target[n] = state.astype(target.dtype)
            return carry

        lax.fori_loop(0, 16, step, 0, unroll=2)

    loads[0].wait()
    loads[1].wait()
    block_states(1 - c, s_oth)
    go(remote(s_oth, s_par, sp_s, sp_r, mate_at(1)))
    block_states(c, s_own)

    def ring(hh, way, step):
        slot = (z + (NZ - step if way == 0 else step)) % NZ
        to = place(x, up(1 if way == 0 else NZ - 1), c)
        return remote(
            kv.at[slot, hh], kv.at[slot, hh], ag_s.at[hh, way, step], ag_r.at[hh, way, step], to
        )

    def ring_got(hh, way, distance):
        slot = (z + (NZ - distance if way == 0 else distance)) % NZ
        to = place(x, up(1 if way == 0 else NZ - 1), c)
        return remote(
            kv.at[slot, hh], kv.at[slot, hh],
            ag_s.at[hh, way, distance - 1], ag_r.at[hh, way, distance - 1], to,
        )

    def reach(hh, way):
        return 4 if way == hh else 3

    def start_ring(hh):
        for sel in range(2):
            kv_own(hh, sel).wait()
            for p in (1, 2, 3):
                kv_quad(hh, sel, p).wait_recv()
        for way in range(2):
            go(ring(hh, way, 0))

    start_ring(0)

    remote(dt.at[c], dt.at[c], d_s, d_r, mate_at(1)).wait_recv()
    remote(s_oth, s_par, sp_s, sp_r, mate_at(1)).wait_recv()
    first = c == 0
    chd[z] = dt[0] + dt[1]

    def chip_state(n, carry):
        h = head_of(n, c)
        later = jnp.exp(dt[1, pl.ds(h, 1), :])
        own, par = s_own[n], s_par[n].astype(F32)
        earlier_state = jnp.where(first, own, par)
        later_state = jnp.where(first, par, own)
        ssend[n // 2, n % 2] = (later * earlier_state + later_state).astype(BF16)
        s_own[n] = earlier_state
        return carry

    lax.fori_loop(0, 16, chip_state, 0, unroll=2)
    sgot[z] = ssend[z]

    def chip_decay(k):
        return remote(chd.at[z], chd.at[z], cd_s.at[k - 1], cd_r.at[k - 1], place(x, up(k), c))

    def chip_decay_got(k):
        slot = up(NZ - k)
        return remote(chd.at[slot], chd.at[slot], cd_s.at[k - 1], cd_r.at[k - 1], place(x, up(k), c))

    def state_move(k):
        return remote(
            ssend.at[up(k)], sgot.at[z], sa_s.at[k - 1], sa_r.at[k - 1], place(x, up(k), c)
        )

    def state_got(k):
        return remote(
            ssend.at[up(k)], sgot.at[up(NZ - k)], sa_s.at[k - 1], sa_r.at[k - 1], place(x, up(k), c)
        )

    for k in Z_ORDER:
        go(chip_decay(k))
        go(state_move(k))

    q_own.wait()
    for p in (1, 2, 3):
        q_quad(p).wait_recv()
    for qb in range(4):
        for hh in range(2):
            for j in range(4):
                qs[hh, qb // 2, j, (qb % 2) * DH : (qb % 2 + 1) * DH, :] = qx[
                    qb, :, (hh * 4 + j) * DH : (hh * 4 + j + 1) * DH
                ]

    start_ring(1)

    def attend(hh, half, j, slot, keys, own):
        s = lax.dot_general(
            qs[hh, half, j], kv[slot, hh, 0, 0:keys, :], ROWS_BY_ROWS, preferred_element_type=F32
        )
        if own:
            row = lax.broadcasted_iota(jnp.int32, (2 * DH, keys), 0)
            col = lax.broadcasted_iota(jnp.int32, (2 * DH, keys), 1)
            s = jnp.where(row >= col - (keys - 2 * DH), s, MASKED)
        now = jnp.max(s, axis=1, keepdims=True)
        if own:
            new = jnp.broadcast_to(now, (2 * DH, DH))
        else:
            old = top[half, j]
            new = jnp.maximum(old, now)
        spread = jnp.concatenate([new] * (keys // DH), axis=1)
        raised = jnp.exp2((s - spread) * EXP2_SCALE)
        part = raised[:, 0:DH]
        for i in range(1, keys // DH):
            part = part + raised[:, i * DH : (i + 1) * DH]
        summed = jnp.dot(
            raised.astype(BF16), kv[slot, hh, 1, 0:keys, :], preferred_element_type=F32
        )
        if own:
            low[half, j] = part
            acc[half, j] = summed
        else:
            fade = jnp.exp2((old - new) * EXP2_SCALE)
            low[half, j] = low[half, j] * fade + part
            acc[half, j] = acc[half, j] * fade + summed
        top[half, j] = new

    def own_slot(hh):
        def step(j, carry):
            attend(hh, 0, j, z, 2 * DH, True)
            attend(hh, 1, j, z, 4 * DH, True)
            return carry

        lax.fori_loop(0, 4, step, 0)

    def other_slot(hh, slot):
        @pl.when(slot < z)
        def _():
            def step(j, carry):
                attend(hh, 0, j, slot, 2 * DH, False)
                attend(hh, 1, j, slot, 4 * DH, False)
                return carry

            lax.fori_loop(0, 4, step, 0)

        @pl.when(slot > z)
        def _():
            def step(j, carry):
                attend(hh, 1, j, slot, 2 * DH, False)
                return carry

            lax.fori_loop(0, 4, step, 0)

    def ring_step(hh, distance):
        ways = [way for way in range(2) if distance <= reach(hh, way)]
        for way in ways:
            ring_got(hh, way, distance).wait_recv()
            if distance < reach(hh, way):
                go(ring(hh, way, distance))
        if len(ways) == 2:
            def step(way, carry):
                other_slot(hh, (z + NZ - distance + 2 * distance * way) % NZ)
                return carry

            lax.fori_loop(0, 2, step, 0)
        else:
            other_slot(hh, (z + (NZ - distance if ways[0] == 0 else distance)) % NZ)

    def finish_heads(hh):
        for half in range(2):
            def step(j, carry):
                total = jnp.sum(low[half, j], axis=1, keepdims=True)
                result = (acc[half, j] / total).astype(BF16)
                ob[hh, 2 * half, :, block(j)] = result[0:DH]
                ob[hh, 2 * half + 1, :, block(j)] = result[DH:]
                return carry

            lax.fori_loop(0, 4, step, 0)
        for p in (2, 3, 1):
            go(out_quad(hh, p))
        out_own(hh).start()

    def out_quad(hh, p):
        return remote(
            ob.at[hh, mate_quad(p)], attn_out.at[:, wide(quad * 2 + hh, 512)],
            o_s.at[hh, p], o_r.at[hh, p], mate_at(p),
        )

    def out_got(hh, p):
        return remote(
            ob.at[hh, mate_quad(p)], attn_out.at[:, wide(mate_quad(p) * 2 + hh, 512)],
            o_s.at[hh, p], o_r.at[hh, p], mate_at(p),
        )

    def out_own(hh):
        return pltpu.make_async_copy(
            ob.at[hh, quad], attn_out.at[:, wide(quad * 2 + hh, 512)], o_r.at[hh, 0]
        )

    def inner_heads():
        def step(h, carry):
            queries = silu(qlv[:, block(h)].astype(F32)).astype(BF16)
            qlv[:, block(h)] = queries
            scores = lax.dot_general(
                queries, klv[:, block(h)], ROWS_BY_ROWS, preferred_element_type=F32
            )
            spread = column(h) - ct[pl.ds(h, 1), :]
            damping = jnp.exp(jnp.where(t_row >= t_col, spread, MASKED))
            damped = (scores * damping).astype(BF16)
            lin[:, block(h)] = jnp.dot(damped, vlv[:, block(h)], preferred_element_type=F32)
            return carry

        lax.fori_loop(0, LHEADS, step, 0, unroll=2)

    t_move = remote(fin, t0, t_s, t_r, mate_at(2))
    so_move = remote(fin.at[0], state_out.at[0], so_s, so_r.at[0], mate_at(2))
    so_own = pltpu.make_async_copy(fin.at[1], state_out.at[0], so_r.at[1])

    def enter_move(k):
        return remote(eout.at[up(k)], egot.at[z], eo_s.at[k - 1], eo_r.at[k - 1], place(x, up(k), c))

    def enter_got(k):
        return remote(
            eout.at[up(k)], egot.at[up(NZ - k)], eo_s.at[k - 1], eo_r.at[k - 1], place(x, up(k), c)
        )

    def owner():
        for k in Z_ORDER:
            chip_decay_got(k).wait_recv()
            state_got(k).wait_recv()

        @pl.when(x == 0)
        def _():
            st_own.wait()
            st_move.wait_recv()
            fin[...] = stin[...]

        @pl.when(x == 1)
        def _():
            t_move.wait_recv()
            fin[...] = t0[...]

        for k in range(2):
            state = fin[k]
            for zi in range(NZ):
                eout[zi, k] = state.astype(BF16)
                decay = jnp.exp(chd[zi, pl.ds(16 * k + 2 * z + c, 1), :])
                state = decay * state + sgot[zi, k].astype(F32)
            fin[k] = state

        @pl.when(x == 0)
        def _():
            t_move.start()

        @pl.when(x == 1)
        def _():
            so_move.start()
            so_own.start()

        for k in Z_ORDER:
            go(enter_move(k))
        egot[z] = eout[z]

    def pair_enter():
        for k in Z_ORDER:
            enter_got(k).wait_recv()

        def step(n, carry):
            h = head_of(n, c)
            entering = egot[n // 2, n % 2]
            after = (jnp.exp(dt[0, pl.ds(h, 1), :]) * entering.astype(F32) + s_own[n]).astype(BF16)
            ent[c, n] = jnp.where(first, entering, after)
            esend[n] = jnp.where(first, after, entering)
            return carry

        lax.fori_loop(0, 16, step, 0, unroll=2)
        go(enter_pair)

    enter_pair = remote(esend, ent.at[c], ep_s, ep_r, mate_at(1))
    enter_pair_got = remote(esend, ent.at[1 - c], ep_s, ep_r, mate_at(1))

    def lightning_end():
        sq[...] = jnp.zeros_like(sq)

        def carried(parity):
            def step(n, carry):
                h = head_of(n, parity)
                reached = jnp.dot(qlv[:, block(h)], ent[parity, n], preferred_element_type=F32)
                mixed = lin[:, block(h)] + jnp.exp(column(h)) * reached
                lin[:, block(h)] = mixed
                sq[...] += mixed * mixed
                return carry

            lax.fori_loop(0, 16, step, 0, unroll=2)

        carried(c)
        enter_pair_got.wait_recv()
        carried(1 - c)
        mean = jnp.sum(sq[...], axis=1, keepdims=True) / (LHEADS * DH)
        factor = jnp.broadcast_to(lax.rsqrt(mean + NORM_EPS), (DH, DH))

        def gated(h, carry):
            gate = 1.0 / (1.0 + jnp.exp(-gtv[:, block(h)].astype(F32)))
            row = lin[:, block(h)] * factor * gain_in[:, block(h)] * gate
            qlv[:, block(h)] = row.astype(BF16)
            return carry

        lax.fori_loop(0, LHEADS, gated, 0, unroll=2)
        light_copy.start()

    light_copy = pltpu.make_async_copy(qlv, light_out, out_s)

    own_slot(0)
    ring_step(0, 1)
    loads[2].wait()
    inner_heads()
    ring_step(0, 2)
    owner()
    ring_step(0, 3)
    ring_step(0, 4)
    finish_heads(0)
    own_slot(1)
    ring_step(1, 1)
    ring_step(1, 2)
    pair_enter()
    ring_step(1, 3)
    loads[3].wait()
    lightning_end()
    ring_step(1, 4)
    finish_heads(1)

    for hh in range(2):
        out_own(hh).wait()
        for p in (1, 2, 3):
            out_got(hh, p).wait_recv()
    light_copy.wait()

    @pl.when(x == 0)
    def _():
        so_move.wait_recv()
        t_move.wait_send()

    @pl.when(x == 1)
    def _():
        st_move.wait_send()
        so_own.wait()
        so_move.wait_send()

    for copy in sends:
        copy.wait_send()


def shards(*arrays):
    (query_lin, key_lin, value_lin, log_decay, out_gate, norm_gain, state_in, query_soft, key_soft,
     value_soft) = arrays
    rows, width = query_lin.shape
    hbm = pl.BlockSpec(memory_space=pl.ANY)
    vmem = pl.BlockSpec(memory_space=pltpu.VMEM)
    dma = pltpu.SemaphoreType.DMA
    state = (DH, DH)
    return pl.pallas_call(
        kernel,
        out_shape=(
            jax.ShapeDtypeStruct((rows, width), BF16),
            jax.ShapeDtypeStruct(state_in.shape, F32),
            jax.ShapeDtypeStruct((rows, width), BF16),
        ),
        in_specs=[hbm, hbm, hbm, vmem, hbm, vmem, hbm, hbm, hbm, hbm],
        out_specs=(hbm, hbm, hbm),
        scratch_shapes=[
            pltpu.VMEM((NZ, 2, 2, 512, DH), BF16),
            pltpu.VMEM((4, rows, 1024), BF16),
            pltpu.VMEM((2, 2, 4, 256, DH), BF16),
            pltpu.VMEM((2, 4, 256, DH), F32),
            pltpu.VMEM((2, 4, 256, DH), F32),
            pltpu.VMEM((2, 4, 256, DH), F32),
            pltpu.VMEM((2, 4, rows, 512), BF16),
            pltpu.VMEM((rows, width), BF16),
            pltpu.VMEM((rows, width), BF16),
            pltpu.VMEM((rows, width), BF16),
            pltpu.VMEM((rows, width), BF16),
            pltpu.VMEM((rows, width), F32),
            pltpu.VMEM((LHEADS, DH), F32),
            pltpu.VMEM((DH, LHEADS), F32),
            pltpu.VMEM((16,) + state, F32),
            pltpu.VMEM((16,) + state, BF16),
            pltpu.VMEM((16,) + state, BF16),
            pltpu.VMEM((NZ, 2) + state, BF16),
            pltpu.VMEM((NZ, 2) + state, BF16),
            pltpu.VMEM((NZ, 2) + state, BF16),
            pltpu.VMEM((NZ, 2) + state, BF16),
            pltpu.VMEM((2, 16) + state, BF16),
            pltpu.VMEM((16,) + state, BF16),
            pltpu.VMEM((2,) + state, F32),
            pltpu.VMEM((2,) + state, F32),
            pltpu.VMEM((2,) + state, F32),
            pltpu.VMEM((2, LHEADS, DH), F32),
            pltpu.VMEM((NZ, LHEADS, DH), F32),
            pltpu.VMEM(state, F32),
            dma((4,)),
            dma((2, 2, 4)), dma((2, 2, 4)),
            dma((4,)), dma((4,)),
            dma, dma((2,)),
            dma, dma,
            dma, dma,
            dma((7,)), dma((7,)),
            dma((7,)), dma((7,)),
            dma((7,)), dma((7,)),
            dma, dma,
            dma, dma((2,)),
            dma, dma,
            dma((2, 2, 4)), dma((2, 2, 4)),
            dma((2, 4)), dma((2, 4)),
            dma,
        ],
        compiler_params=pltpu.CompilerParams(
            collective_id=0, has_side_effects=True, vmem_limit_bytes=48 * 2**20
        ),
        name="window",
    )(
        query_lin, key_lin, value_lin, log_decay, out_gate, norm_gain.reshape(1, width), state_in,
        query_soft, key_soft, value_soft,
    )


def solution(mesh):
    rows = P(("dp", "seq"), None)
    states = P(("dp", "seq"), None, None)
    return jax.shard_map(
        shards,
        mesh=mesh,
        in_specs=(rows, rows, rows, rows, rows, P(), states, rows, rows, rows),
        out_specs=(rows, states, rows),
        check_vma=False,
    )
```

time: 774 us -> 125 us (0.16)
  waiting for transfers between devices: 462 us -> 0 us
  Pallas kernels: 0 us -> 114 us
  other arithmetic: 87.7 us -> 0 us
  blocking collectives: 81.9 us -> 0 us
  matrix products: 43.3 us -> 0 us
  local copies, waits for them, and re-layouts: 46.8 us -> 9.8 us
  starting transfers between devices: 29.5 us -> 0 us
  between operations: 15.1 us -> 0.66 us
    psum x1 -> x0, waiting for transfers between devices: 213 us -> none  [spread_2(): return lax.psum(jnp.where(mine, x, jnp.zeros_like(x)), axis)]
    all_gather x2 -> x0, waiting for transfers between devices: 179 us -> none  [the longest x1 179 us: carried_in_2(): everything = jax.tree.map(lambda part: lax.all_gather(part, axis), x)]
    pallas_call x0 -> x1, Pallas kernels: none -> 114 us  [shards(): pl.pallas_call(kernel, out_shape=(jax.ShapeDtypeStruct((rows, width), BF1...]
    unnamed x1 -> x0, blocking collectives: 81.9 us -> none
    select_n x65 -> x0, other arithmetic: 71.8 us -> none  [the longest x64 67.8 us: lap(): return jax.tree.map(lambda a, b: jnp.where(reached, a, b), new, before)]
    all_to_all x4 -> x0, waiting for transfers between devices: 70.1 us -> none  [the longest x1 36.9 us: shards(): lax.all_to_all(spread_heads(value_soft), 'seq', split_axis=1, concat_axis...]
    dot_general x20 -> x0, matrix products: 43.3 us -> none  [the longest x8 13.9 us: shards(): jnp.einsum('hts,sd->thd', raised, value_heads[:stop_row], preferred_eleme...]
    all_to_all x4 -> x0, starting transfers between devices: 29.4 us -> none  [the longest x1 11.1 us: shards(): lax.all_to_all(spread_heads(value_soft), 'seq', split_axis=1, concat_axis...]
  transfers between devices with their start and end apart: 7 -> 0, of which waited for: 4 -> 0; matrix products, arithmetic and copies ran while one was open for 21% -> 0% of each run, Pallas kernels for 0% -> 0%
where the time goes in v1:
time: 125 us; the launch traced here: 124 us
  Pallas kernels  114 us (91%)
  local copies, waits for them, and re-layouts  9.8 us (8%)
    pallas_call x1, Pallas kernels, shards(): pl.pallas_call(kernel, out_shape=(jax.ShapeDtypeStruct((rows, width), BF1...  114 us
    unnamed x18, local copies, waits for them, and re-layouts  9.8 us

profile of v1, /device:TPU:1, one launch (start us, length us, event | category | flops | bytes accessed | tf_op | source)
XLA Modules:
  0.0 124.4 jit_solution(6349990330098105495)
XLA Ops:
  0.6 0.0 copy-start.6
  0.6 0.8 copy.13.ld_in
  1.5 0.0 copy-done.6
  1.5 0.0 copy-start
  1.5 1.2 copy-done
  2.7 0.0 copy-start.1
  2.7 1.2 copy-done.1
  3.9 0.0 copy-start.2
  3.9 1.2 copy-done.2
  5.1 0.0 copy-start.3
  5.1 0.9 copy-done.3
  6.1 0.0 copy-start.4
  6.1 0.9 copy-done.4
  7.0 0.0 copy-start.5
  7.0 0.8 copy-done.5
  7.9 113.9 %window.1 = (bf16[128,4096]{1,0:T(8,128)(2,1)S(1)}, f32[1,128,128]{2,1,0:T(8,128)S(1)}, bf16[128,4096]{1,0:T(8,128)(2,1)S(1)}) custom-call(bf16[128,4096]{1,0:T(8,128)(2,1)S(1)} %copy-done, bf16[128,4096]{1,0:T(8,128)(2,1)S(1)} %copy-done.1, bf16[128,4096]{1,0:T(8,128)(2,1)S(1)} %copy-done.2, bf16[128,32]{1,0:T(8,128)(2,1)S(1)} %copy.13.ld_in, ...), custom_call_target="tpu_custom_call" | custom-call | tf_op jit(solution)/shard_map/window/pallas_call | solution.py:519
  121.8 1.0 copy.17
  122.8 0.6 copy.18
  123.4 1.0 copy.19
Async XLA Ops:
  0.6 0.8 copy-start.6
  1.5 1.2 copy-start
  2.7 1.2 copy-start.1
  3.9 1.2 copy-start.2
  5.1 0.9 copy-start.3
  6.1 0.9 copy-start.4
  7.0 0.8 copy-start.5

commit v2 on v1

v2 whole, which is shorter than its diff:
```python
import functools
import math

import jax
import jax.numpy as jnp
from jax import lax
from jax.experimental import pallas as pl
from jax.experimental.pallas import tpu as pltpu
from jax.sharding import PartitionSpec as P

DH = 128
NZ = 8
LHEADS = 32
NORM_EPS = 1e-6
SCALE = DH ** (-0.5)
EXP2_SCALE = SCALE * math.log2(math.e)
MASKED = -1e30
MESH = pl.DeviceIdType.MESH
F32 = jnp.float32
BF16 = jnp.bfloat16
UNROLL = 4
ROWS_BY_ROWS = (((1,), (1,)), ((), ()))
COLS_BY_COLS = (((0,), (0,)), ((), ()))
Z_ORDER = (4, 3, 5, 2, 6, 1, 7)


def place(x, z, c):
    return (x * NZ + z) * 2 + c


def block(index):
    return pl.ds(pl.multiple_of(index * DH, DH), DH)


def wide(index, width):
    return pl.ds(pl.multiple_of(index * width, width), width)


def kernel(
    ql_in, kl_in, vl_in, ld_in, gate_in, gain_in, state_in, q_in, k_in, v_in,
    light_out, state_out, attn_out,
    kv, qx, acc, top, low, ob, vsv, vtl,
    qlv, klv, vlv, gtv, lin, ct, cv, s_own, s_oth, s_par, ssend, sgot, eout, egot, ent, esend, gf,
    stin, t0, fin, dt, chd, sq,
    lsem, kvs, kvr, qsend, qrecv, st_s, st_r, d_s, d_r, sp_s, sp_r, cd_s, cd_r, sa_s, sa_r,
    eo_s, eo_r, t_s, t_r, so_s, so_r, ep_s, ep_r, ag_s, ag_r, o_s, o_r, out_s,
):
    me = lax.axis_index("seq")
    x = me // (2 * NZ)
    z = (me // 2) % NZ
    c = me % 2
    quad = x * 2 + c
    mates = {1: (x, 1 - c), 2: (1 - x, c), 3: (1 - x, 1 - c)}

    def mate_quad(p):
        mx, mc = mates[p]
        return mx * 2 + mc

    def mate_at(p):
        mx, mc = mates[p]
        return place(mx, z, mc)

    def up(k):
        return (z + k) % NZ

    def remote(src, dst, send, recv, to):
        return pltpu.make_async_remote_copy(
            src_ref=src, dst_ref=dst, send_sem=send, recv_sem=recv,
            device_id={"seq": to}, device_id_type=MESH,
        )

    sends = []

    def go(copy):
        copy.start()
        sends.append(copy)

    barrier = pltpu.get_barrier_semaphore()
    peers = [mate_at(p) for p in (1, 2, 3)] + [place(x, up(k), c) for k in range(1, NZ)]
    for peer in peers:
        pl.semaphore_signal(barrier, inc=1, device_id={"seq": peer}, device_id_type=MESH)

    loads = [
        pltpu.make_async_copy(v_in, vsv, lsem.at[0]),
        pltpu.make_async_copy(kl_in, klv, lsem.at[1]),
        pltpu.make_async_copy(vl_in, vlv, lsem.at[2]),
        pltpu.make_async_copy(ql_in, qlv, lsem.at[3]),
        pltpu.make_async_copy(gate_in, gtv, lsem.at[4]),
    ]
    for load in loads:
        load.start()

    def head_of(n, parity):
        return 16 * (n % 2) + 2 * (n // 2) + parity

    t_row = lax.broadcasted_iota(jnp.int32, (DH, DH), 0)
    t_col = lax.broadcasted_iota(jnp.int32, (DH, DH), 1)
    tril = jnp.where(t_row >= t_col, 1.0, 0.0).astype(BF16)
    cum = jnp.dot(tril, ld_in[...], preferred_element_type=F32)
    cv[...] = cum
    cum_t = jnp.transpose(cum)
    ct[...] = cum_t
    dt[c] = jnp.broadcast_to(cum_t[:, DH - 1 :], (LHEADS, DH))

    loads[0].wait()
    for g in range(8):
        vtl[g] = jnp.transpose(vsv[:, g * DH : (g + 1) * DH])

    pl.semaphore_wait(barrier, len(peers))

    def kv_quad(hh, sel, p):
        head = mate_quad(p) * 2 + hh
        src = vtl.at[head] if sel else k_in.at[:, block(head)]
        return remote(
            src, kv.at[z, hh, x, sel, block(c), :], kvs.at[hh, sel, p], kvr.at[hh, sel, p], mate_at(p)
        )

    def kv_quad_got(hh, sel, p):
        head = mate_quad(p) * 2 + hh
        src = vtl.at[head] if sel else k_in.at[:, block(head)]
        mx, mc = mates[p]
        return remote(
            src, kv.at[z, hh, mx, sel, block(mc), :], kvs.at[hh, sel, p], kvr.at[hh, sel, p], mate_at(p)
        )

    def kv_own(hh, sel):
        head = quad * 2 + hh
        src = vtl.at[head] if sel else k_in.at[:, block(head)]
        return pltpu.make_async_copy(src, kv.at[z, hh, x, sel, block(c), :], kvr.at[hh, sel, 0])

    for hh in range(2):
        for sel in range(2):
            go(kv_quad(hh, sel, 1))
            kv_own(hh, sel).start()
    for hh in range(2):
        for p in (2, 3):
            for sel in range(2):
                go(kv_quad(hh, sel, p))
    go(remote(dt.at[c], dt.at[c], d_s, d_r, mate_at(1)))

    def ring(hh, way, step, half):
        slot = (z + (NZ - step if way == 0 else step)) % NZ
        to = place(x, up(1 if way == 0 else NZ - 1), c)
        piece = kv.at[slot, hh, x if half == 0 else 1 - x]
        return remote(piece, piece, ag_s.at[hh, way, step, half], ag_r.at[hh, way, step, half], to)

    def ring_got(hh, way, distance, half):
        slot = (z + (NZ - distance if way == 0 else distance)) % NZ
        to = place(x, up(1 if way == 0 else NZ - 1), c)
        piece = kv.at[slot, hh, x if half == 0 else 1 - x]
        step = distance - 1
        return remote(piece, piece, ag_s.at[hh, way, step, half], ag_r.at[hh, way, step, half], to)

    def reach(hh, way):
        return 4 if way == hh else 3

    def start_ring(hh, half):
        for sel in range(2):
            if half == 0:
                kv_own(hh, sel).wait()
                kv_quad_got(hh, sel, 1).wait_recv()
            else:
                kv_quad_got(hh, sel, 2).wait_recv()
                kv_quad_got(hh, sel, 3).wait_recv()
        for way in range(2):
            go(ring(hh, way, 0, half))

    def pump(hh, distance):
        for half in range(2):
            for way in range(2):
                if distance <= reach(hh, way):
                    ring_got(hh, way, distance, half).wait_recv()
                    if distance < reach(hh, way):
                        go(ring(hh, way, distance, half))

    def column(h):
        lanes = lax.broadcasted_iota(jnp.int32, (DH, LHEADS), 1)
        return jnp.sum(jnp.where(lanes == h, cv[...], 0.0), axis=1, keepdims=True)

    def silu(u):
        return u / (1.0 + jnp.exp(-u))

    def block_states(parity, target):
        def step(n, carry):
            h = head_of(n, parity)
            keys = (silu(klv[:, block(h)].astype(F32)) * SCALE).astype(BF16)
            klv[:, block(h)] = keys
            col = column(h)
            decayed = (keys.astype(F32) * jnp.exp(col[DH - 1 :, :] - col)).astype(BF16)
            state = lax.dot_general(
                decayed, vlv[:, block(h)], COLS_BY_COLS, preferred_element_type=F32
            )
            target[n] = state.astype(target.dtype)
            return carry

        lax.fori_loop(0, 16, step, 0, unroll=4)

    start_ring(0, 0)
    start_ring(1, 0)
    loads[1].wait()
    loads[2].wait()
    block_states(1 - c, s_oth)
    go(remote(s_oth, s_par, sp_s, sp_r, mate_at(1)))
    start_ring(0, 1)
    block_states(c, s_own)
    start_ring(1, 1)

    def q_quad(hh, p):
        return remote(
            q_in.at[:, wide(mate_quad(p) * 2 + hh, 512)], qx.at[hh, quad],
            qsend.at[hh, p], qrecv.at[hh, p], mate_at(p),
        )

    def q_quad_got(hh, p):
        return remote(
            q_in.at[:, wide(mate_quad(p) * 2 + hh, 512)], qx.at[hh, mate_quad(p)],
            qsend.at[hh, p], qrecv.at[hh, p], mate_at(p),
        )

    def q_own(hh):
        return pltpu.make_async_copy(
            q_in.at[:, wide(quad * 2 + hh, 512)], qx.at[hh, quad], qrecv.at[hh, 0]
        )

    for hh in range(2):
        for p in (2, 3, 1):
            go(q_quad(hh, p))
        q_own(hh).start()

    st_own = pltpu.make_async_copy(state_in.at[0], stin.at[0], st_r.at[0])
    st_move = remote(state_in.at[0], stin.at[1], st_s, st_r.at[1], mate_at(2))

    @pl.when(x == 0)
    def _():
        st_own.start()

    @pl.when(x == 1)
    def _():
        st_move.start()

    remote(dt.at[c], dt.at[1 - c], d_s, d_r, mate_at(1)).wait_recv()
    remote(s_oth, s_par, sp_s, sp_r, mate_at(1)).wait_recv()
    first = c == 0
    chd[z] = dt[0] + dt[1]

    def chip_state(n, carry):
        h = head_of(n, c)
        later = jnp.exp(dt[1, pl.ds(h, 1), :])
        own, par = s_own[n], s_par[n].astype(F32)
        earlier_state = jnp.where(first, own, par)
        later_state = jnp.where(first, par, own)
        ssend[n // 2, n % 2] = (later * earlier_state + later_state).astype(BF16)
        s_own[n] = earlier_state
        return carry

    lax.fori_loop(0, 16, chip_state, 0, unroll=2)
    sgot[z] = ssend[z]

    def chip_decay(k):
        return remote(chd.at[z], chd.at[z], cd_s.at[k - 1], cd_r.at[k - 1], place(x, up(k), c))

    def chip_decay_got(k):
        slot = up(NZ - k)
        return remote(chd.at[slot], chd.at[slot], cd_s.at[k - 1], cd_r.at[k - 1], place(x, up(k), c))

    def state_move(k):
        return remote(
            ssend.at[up(k)], sgot.at[z], sa_s.at[k - 1], sa_r.at[k - 1], place(x, up(k), c)
        )

    def state_got(k):
        return remote(
            ssend.at[up(k)], sgot.at[up(NZ - k)], sa_s.at[k - 1], sa_r.at[k - 1], place(x, up(k), c)
        )

    for k in Z_ORDER:
        go(chip_decay(k))
        go(state_move(k))

    def attend(hh, half, j, slot, both, own):
        heads = pl.ds(pl.multiple_of(j * DH, DH), DH)
        queries = jnp.concatenate([qx[hh, 2 * half, :, heads], qx[hh, 2 * half + 1, :, heads]], axis=0)
        parts = (0, 1) if both else (0,)
        keys = jnp.concatenate([kv[slot, hh, i, 0] for i in parts], axis=0)
        values = jnp.concatenate(
            [kv[slot, hh, i, 1, b * DH : (b + 1) * DH, :] for i in parts for b in range(2)], axis=1
        )
        s = lax.dot_general(keys, queries, ROWS_BY_ROWS, preferred_element_type=F32)
        if own:
            count = s.shape[0]
            key = lax.broadcasted_iota(jnp.int32, s.shape, 0) - (count - 2 * DH)
            query = lax.broadcasted_iota(jnp.int32, s.shape, 1)
            s = jnp.where(key <= query, s, MASKED)
        row = pl.ds(half * 4 + j, 1)
        new = jnp.max(s, axis=0, keepdims=True)
        if not own:
            old = top[hh, row, :]
            new = jnp.maximum(old, new)
        raised = jnp.exp2((s - new) * EXP2_SCALE)
        part = jnp.sum(raised, axis=0, keepdims=True)
        summed = jnp.dot(values, raised.astype(BF16), preferred_element_type=F32)
        if own:
            low[hh, row, :] = part
            acc[hh, half, j] = summed
        else:
            fade = jnp.exp2((old - new) * EXP2_SCALE)
            low[hh, row, :] = low[hh, row, :] * fade + part
            acc[hh, half, j] = acc[hh, half, j] * fade + summed
        top[hh, row, :] = new

    def over_heads(body):
        def step(j, carry):
            body(j)
            return carry

        lax.fori_loop(0, 4, step, 0, unroll=UNROLL)

    def own_slot(hh):
        def body(j):
            attend(hh, 0, j, z, False, True)
            attend(hh, 1, j, z, True, True)

        over_heads(body)

    def other_slot(hh, slot):
        @pl.when(slot < z)
        def _():
            def body(j):
                attend(hh, 0, j, slot, False, False)
                attend(hh, 1, j, slot, True, False)

            over_heads(body)

        @pl.when(slot > z)
        def _():
            over_heads(lambda j: attend(hh, 1, j, slot, False, False))

    def process(hh, distance):
        ways = [way for way in range(2) if distance <= reach(hh, way)]
        if len(ways) == 2:
            def step(way, carry):
                other_slot(hh, (z + NZ - distance + 2 * distance * way) % NZ)
                return carry

            lax.fori_loop(0, 2, step, 0)
        else:
            other_slot(hh, (z + (NZ - distance if ways[0] == 0 else distance)) % NZ)

    def finish_heads(hh):
        for half in range(2):
            def step(j, carry):
                scale = 1.0 / low[hh, pl.ds(half * 4 + j, 1), :]
                result = jnp.transpose(acc[hh, half, j] * scale).astype(BF16)
                ob[hh, 2 * half, :, block(j)] = result[0:DH]
                ob[hh, 2 * half + 1, :, block(j)] = result[DH:]
                return carry

            lax.fori_loop(0, 4, step, 0, unroll=2)
        for p in (2, 3, 1):
            go(out_quad(hh, p))
        out_own(hh).start()

    def out_quad(hh, p):
        return remote(
            ob.at[hh, mate_quad(p)], attn_out.at[:, wide(quad * 2 + hh, 512)],
            o_s.at[hh, p], o_r.at[hh, p], mate_at(p),
        )

    def out_got(hh, p):
        return remote(
            ob.at[hh, mate_quad(p)], attn_out.at[:, wide(mate_quad(p) * 2 + hh, 512)],
            o_s.at[hh, p], o_r.at[hh, p], mate_at(p),
        )

    def out_own(hh):
        return pltpu.make_async_copy(
            ob.at[hh, quad], attn_out.at[:, wide(quad * 2 + hh, 512)], o_r.at[hh, 0]
        )

    def queries_here(hh):
        q_own(hh).wait()
        for p in (1, 2, 3):
            q_quad_got(hh, p).wait_recv()

    def inner_heads(begin, end):
        def step(h, carry):
            queries = silu(qlv[:, block(h)].astype(F32)).astype(BF16)
            qlv[:, block(h)] = queries
            scores = lax.dot_general(
                queries, klv[:, block(h)], ROWS_BY_ROWS, preferred_element_type=F32
            )
            spread = column(h) - ct[pl.ds(h, 1), :]
            damping = jnp.exp(jnp.where(t_row >= t_col, spread, MASKED))
            damped = (scores * damping).astype(BF16)
            lin[:, block(h)] = jnp.dot(damped, vlv[:, block(h)], preferred_element_type=F32)
            return carry

        lax.fori_loop(begin, end, step, 0, unroll=4)

    t_move = remote(fin, t0, t_s, t_r, mate_at(2))
    so_move = remote(fin.at[0], state_out.at[0], so_s, so_r.at[0], mate_at(2))
    so_own = pltpu.make_async_copy(fin.at[1], state_out.at[0], so_r.at[1])

    def enter_move(k, part):
        return remote(
            eout.at[up(k), part], egot.at[z, part],
            eo_s.at[part, k - 1], eo_r.at[part, k - 1], place(x, up(k), c),
        )

    def enter_got(k, part):
        return remote(
            eout.at[up(k), part], egot.at[up(NZ - k), part],
            eo_s.at[part, k - 1], eo_r.at[part, k - 1], place(x, up(k), c),
        )

    def prefix():
        for k in range(2):
            state = fin[k]
            for zi in range(NZ):
                eout[zi, k] = state.astype(BF16)
                decay = jnp.exp(chd[zi, pl.ds(16 * k + 2 * z + c, 1), :])
                state = decay * state + sgot[zi, k].astype(F32)
            fin[k] = state

    def states_here():
        for k in Z_ORDER:
            chip_decay_got(k).wait_recv()
            state_got(k).wait_recv()

    def owner_0():
        @pl.when(x == 0)
        def _():
            st_own.wait()
            st_move.wait_recv()
            fin[...] = stin[...]
            prefix()
            t_move.start()

    def owner_1():
        @pl.when(x == 1)
        def _():
            t_move.wait_recv()
            fin[...] = t0[...]
            prefix()
            so_move.start()
            so_own.start()

    def enter_send(part):
        for k in Z_ORDER:
            go(enter_move(k, part))
        egot[z, part] = eout[z, part]

    def pair_enter(part):
        for k in Z_ORDER:
            enter_got(k, part).wait_recv()

        def step(zi, carry):
            h = 16 * part + 2 * zi + c
            entering = egot[zi, part]
            after = jnp.exp(dt[0, pl.ds(h, 1), :]) * entering.astype(F32) + s_own[2 * zi + part]
            after = after.astype(BF16)
            ent[c, part, zi] = jnp.where(first, entering, after)
            esend[part, zi] = jnp.where(first, after, entering)
            return carry

        lax.fori_loop(0, NZ, step, 0, unroll=2)
        go(enter_pair(part))

    def enter_pair(part):
        return remote(esend.at[part], ent.at[c, part], ep_s.at[part], ep_r.at[part], mate_at(1))

    def enter_pair_got(part):
        return remote(esend.at[part], ent.at[1 - c, part], ep_s.at[part], ep_r.at[part], mate_at(1))

    def carried(parity, part):
        def step(zi, carry):
            h = 16 * part + 2 * zi + parity
            reached = jnp.dot(qlv[:, block(h)], ent[parity, part, zi], preferred_element_type=F32)
            mixed = lin[:, block(h)] + jnp.exp(column(h)) * reached
            lin[:, block(h)] = mixed
            sq[...] += mixed * mixed
            return carry

        lax.fori_loop(0, NZ, step, 0, unroll=4)

    def gates():
        def step(h, carry):
            gate = 1.0 / (1.0 + jnp.exp(-gtv[:, block(h)].astype(F32)))
            gf[:, block(h)] = gain_in[:, block(h)] * gate
            return carry

        lax.fori_loop(0, LHEADS, step, 0, unroll=4)

    def gated_heads():
        mean = jnp.sum(sq[...], axis=1, keepdims=True) / (LHEADS * DH)
        factor = jnp.broadcast_to(lax.rsqrt(mean + NORM_EPS), (DH, DH))

        def gated(h, carry):
            qlv[:, block(h)] = (lin[:, block(h)] * factor * gf[:, block(h)]).astype(BF16)
            return carry

        lax.fori_loop(0, LHEADS, gated, 0, unroll=4)
        light_copy.start()

    light_copy = pltpu.make_async_copy(qlv, light_out, out_s)

    loads[3].wait()
    inner_heads(0, 16)
    pump(0, 1)
    inner_heads(16, 32)
    pump(1, 1)
    queries_here(0)
    own_slot(0)
    process(0, 1)
    queries_here(1)
    own_slot(1)
    states_here()
    owner_0()
    process(1, 1)
    pump(0, 2)
    pump(1, 2)
    owner_1()
    enter_send(0)
    process(0, 2)
    pump(0, 3)
    process(1, 2)
    pump(1, 3)
    enter_send(1)
    process(0, 3)
    loads[4].wait()
    gates()
    pump(0, 4)
    process(0, 4)
    finish_heads(0)
    process(1, 3)
    pair_enter(0)
    sq[...] = jnp.zeros_like(sq)
    carried(c, 0)
    pump(1, 4)
    process(1, 4)
    finish_heads(1)
    enter_pair_got(0).wait_recv()
    carried(1 - c, 0)
    pair_enter(1)
    carried(c, 1)
    enter_pair_got(1).wait_recv()
    carried(1 - c, 1)
    gated_heads()

    for hh in range(2):
        out_own(hh).wait()
        for p in (1, 2, 3):
            out_got(hh, p).wait_recv()
    light_copy.wait()

    @pl.when(x == 0)
    def _():
        so_move.wait_recv()
        t_move.wait_send()

    @pl.when(x == 1)
    def _():
        st_move.wait_send()
        so_own.wait()
        so_move.wait_send()

    for copy in sends:
        copy.wait_send()


def shards(*arrays):
    (query_lin, key_lin, value_lin, log_decay, out_gate, norm_gain, state_in, query_soft, key_soft,
     value_soft) = arrays
    rows, width = query_lin.shape
    hbm = pl.BlockSpec(memory_space=pl.ANY)
    vmem = pl.BlockSpec(memory_space=pltpu.VMEM)
    dma = pltpu.SemaphoreType.DMA
    state = (DH, DH)
    return pl.pallas_call(
        kernel,
        out_shape=(
            jax.ShapeDtypeStruct((rows, width), BF16),
            jax.ShapeDtypeStruct(state_in.shape, F32),
            jax.ShapeDtypeStruct((rows, width), BF16),
        ),
        in_specs=[hbm, hbm, hbm, vmem, hbm, vmem, hbm, hbm, hbm, hbm],
        out_specs=(hbm, hbm, hbm),
        scratch_shapes=[
            pltpu.VMEM((NZ, 2, 2, 2, 2 * DH, DH), BF16),
            pltpu.VMEM((2, 4, rows, 512), BF16),
            pltpu.VMEM((2, 2, 4, DH, 2 * DH), F32),
            pltpu.VMEM((2, 8, 2 * DH), F32),
            pltpu.VMEM((2, 8, 2 * DH), F32),
            pltpu.VMEM((2, 4, rows, 512), BF16),
            pltpu.VMEM((rows, 1024), BF16),
            pltpu.VMEM((8, DH, rows), BF16),
            pltpu.VMEM((rows, width), BF16),
            pltpu.VMEM((rows, width), BF16),
            pltpu.VMEM((rows, width), BF16),
            pltpu.VMEM((rows, width), BF16),
            pltpu.VMEM((rows, width), F32),
            pltpu.VMEM((LHEADS, DH), F32),
            pltpu.VMEM((DH, LHEADS), F32),
            pltpu.VMEM((16,) + state, F32),
            pltpu.VMEM((16,) + state, BF16),
            pltpu.VMEM((16,) + state, BF16),
            pltpu.VMEM((NZ, 2) + state, BF16),
            pltpu.VMEM((NZ, 2) + state, BF16),
            pltpu.VMEM((NZ, 2) + state, BF16),
            pltpu.VMEM((NZ, 2) + state, BF16),
            pltpu.VMEM((2, 2, NZ) + state, BF16),
            pltpu.VMEM((2, NZ) + state, BF16),
            pltpu.VMEM((rows, width), F32),
            pltpu.VMEM((2,) + state, F32),
            pltpu.VMEM((2,) + state, F32),
            pltpu.VMEM((2,) + state, F32),
            pltpu.VMEM((2, LHEADS, DH), F32),
            pltpu.VMEM((NZ, LHEADS, DH), F32),
            pltpu.VMEM(state, F32),
            dma((5,)),
            dma((2, 2, 4)), dma((2, 2, 4)),
            dma((2, 4)), dma((2, 4)),
            dma, dma((2,)),
            dma, dma,
            dma, dma,
            dma((7,)), dma((7,)),
            dma((7,)), dma((7,)),
            dma((2, 7)), dma((2, 7)),
            dma, dma,
            dma, dma((2,)),
            dma((2,)), dma((2,)),
            dma((2, 2, 4, 2)), dma((2, 2, 4, 2)),
            dma((2, 4)), dma((2, 4)),
            dma,
        ],
        compiler_params=pltpu.CompilerParams(
            collective_id=0, has_side_effects=True, vmem_limit_bytes=62 * 2**20
        ),
        name="window",
    )(
        query_lin, key_lin, value_lin, log_decay, out_gate, norm_gain.reshape(1, width), state_in,
        query_soft, key_soft, value_soft,
    )


def solution(mesh):
    rows = P(("dp", "seq"), None)
    states = P(("dp", "seq"), None, None)
    return jax.shard_map(
        shards,
        mesh=mesh,
        in_specs=(rows, rows, rows, rows, rows, P(), states, rows, rows, rows),
        out_specs=(rows, states, rows),
        check_vma=False,
    )
```

time: 125 us -> 94.7 us (0.76)
  Pallas kernels: 114 us -> 88.3 us
  local copies, waits for them, and re-layouts: 9.8 us -> 5.4 us
    pallas_call x1, Pallas kernels: 114 us -> 88.3 us  [shards(): pl.pallas_call(kernel, out_shape=(jax.ShapeDtypeStruct((rows, width), BF1...]
    unnamed x18 -> x8, local copies, waits for them, and re-layouts: 9.8 us -> 5.4 us
where the time goes in v2:
time: 94.7 us; the launch traced here: 94.4 us
  Pallas kernels  88.3 us (93%)
  local copies, waits for them, and re-layouts  5.4 us (6%)
    pallas_call x1, Pallas kernels, shards(): pl.pallas_call(kernel, out_shape=(jax.ShapeDtypeStruct((rows, width), BF1...  88.3 us
    unnamed x8, local copies, waits for them, and re-layouts  5.4 us

profile of v2, /device:TPU:1, one launch (start us, length us, event | category | flops | bytes accessed | tf_op | source)
XLA Modules:
  0.0 94.4 jit_solution(1353278063550912698)
XLA Ops:
  0.6 1.4 %copy.13.ld_in = bf16[128,32]{1,0:T(8,128)(2,1)} copy(bf16[128,32]{0,1:T(8,128)(2,1)} %param.13) | data formatting | bytes 16384 | tf_op args[3]
  2.0 88.3 %window.1 = (bf16[128,4096]{1,0:T(8,128)(2,1)}, f32[1,128,128]{2,1,0:T(8,128)}, bf16[128,4096]{1,0:T(8,128)(2,1)}) custom-call(bf16[128,4096]{1,0:T(8,128)(2,1)} %ql_in.1, bf16[128,4096]{1,0:T(8,128)(2,1)} %kl_in.1, bf16[128,4096]{1,0:T(8,128)(2,1)} %vl_in.1, bf16[128,32]{1,0:T(8,128)(2,1)} %copy.13.ld_in, bf16[128,4096]{1,0:T(8,128)(2,1)} %gate_in.1, ...), custom_call_target="tpu_custom_call" | custom-call | tf_op jit(solution)/shard_map/window/pallas_call | solution.py:579
  90.4 0.0 copy-start.1
  90.4 0.0 copy-start
  90.4 2.4 %copy.17 = bf16[128,4096]{1,0:T(8,128)(2,1)} copy(bf16[128,4096]{1,0:T(8,128)(2,1)} %get-tuple-element.6) | data formatting | bytes 2097152
  92.8 0.0 copy-done.1
  92.8 0.6 copy.18
  93.4 0.0 copy-done
  93.4 1.0 %copy.19 = bf16[128,4096]{1,0:T(8,128)(2,1)} copy(bf16[128,4096]{1,0:T(8,128)(2,1)S(1)} %copy-done) | data formatting | bytes 2097152
Async XLA Ops:
  90.4 2.4 %copy-start.1 = (f32[1,128,128]{2,1,0:T(8,128)S(1)}, f32[1,128,128]{2,1,0:T(8,128)}, u32[]{:S(2)}) copy-start(f32[1,128,128]{2,1,0:T(8,128)} %get-tuple-element.7) | copy-start | bytes 196612
  90.4 3.0 %copy-start = (bf16[128,4096]{1,0:T(8,128)(2,1)S(1)}, bf16[128,4096]{1,0:T(8,128)(2,1)}, u32[]{:S(2)}) copy-start(bf16[128,4096]{1,0:T(8,128)(2,1)} %get-tuple-element.8) | copy-start | bytes 3145732

commit v3 on v2

--- a/solution.py
+++ b/solution.py
@@ -37,11 +37,11 @@
 
 
 def kernel(
-    ql_in, kl_in, vl_in, ld_in, gate_in, gain_in, state_in, q_in, k_in, v_in,
+    ql_in, kl_in, vl_in, ld_hbm, gate_in, gain_in, state_in, q_in, k_in, v_in,
     light_out, state_out, attn_out,
     kv, qx, acc, top, low, ob, vsv, vtl,
     qlv, klv, vlv, gtv, lin, ct, cv, s_own, s_oth, s_par, ssend, sgot, eout, egot, ent, esend, gf,
-    stin, t0, fin, dt, chd, sq,
+    stin, t0, fin, dt, chd, sq, ld_in,
     lsem, kvs, kvr, qsend, qrecv, st_s, st_r, d_s, d_r, sp_s, sp_r, cd_s, cd_r, sa_s, sa_r,
     eo_s, eo_r, t_s, t_r, so_s, so_r, ep_s, ep_r, ag_s, ag_r, o_s, o_r, out_s,
 ):
@@ -86,20 +86,21 @@
         pltpu.make_async_copy(vl_in, vlv, lsem.at[2]),
         pltpu.make_async_copy(ql_in, qlv, lsem.at[3]),
         pltpu.make_async_copy(gate_in, gtv, lsem.at[4]),
+        pltpu.make_async_copy(ld_hbm, ld_in, lsem.at[5]),
     ]
-    for load in loads:
-        load.start()
+    for i in (5, 0, 1, 2, 3, 4):
+        loads[i].start()
+    loads[5].wait()
 
     def head_of(n, parity):
         return 16 * (n % 2) + 2 * (n // 2) + parity
 
     t_row = lax.broadcasted_iota(jnp.int32, (DH, DH), 0)
     t_col = lax.broadcasted_iota(jnp.int32, (DH, DH), 1)
-    tril = jnp.where(t_row >= t_col, 1.0, 0.0).astype(BF16)
-    cum = jnp.dot(tril, ld_in[...], preferred_element_type=F32)
-    cv[...] = cum
-    cum_t = jnp.transpose(cum)
+    triu = jnp.where(t_row <= t_col, 1.0, 0.0).astype(BF16)
+    cum_t = jnp.dot(ld_in[...], triu, preferred_element_type=F32)
     ct[...] = cum_t
+    cv[...] = jnp.transpose(cum_t)
     dt[c] = jnp.broadcast_to(cum_t[:, DH - 1 :], (LHEADS, DH))
 
     loads[0].wait()
@@ -151,8 +152,34 @@
         step = distance - 1
         return remote(piece, piece, ag_s.at[hh, way, step, half], ag_r.at[hh, way, step, half], to)
 
-    def reach(hh, way):
-        return 4 if way == hh else 3
+    def reach(way, half):
+        return 4 if way == half else 3
+
+    def later(half):
+        return (x == 1) if half == 0 else (x == 0)
+
+    def goes(way, step, half):
+        if way == 0:
+            needed = jnp.logical_and(z >= step, z < NZ - 1)
+        else:
+            needed = (z + step) % NZ < reach(way, half)
+        return jnp.logical_or(jnp.logical_not(later(half)), needed)
+
+    def comes(way, distance, half):
+        if way == 0:
+            needed = z >= distance
+        else:
+            needed = (z + distance) % NZ < reach(way, half)
+        return jnp.logical_or(jnp.logical_not(later(half)), needed)
+
+    ring_sends = []
+
+    def go_ring(hh, way, step, half):
+        @pl.when(goes(way, step, half))
+        def _():
+            ring(hh, way, step, half).start()
+
+        ring_sends.append((hh, way, step, half))
 
     def start_ring(hh, half):
         for sel in range(2):
@@ -163,15 +190,18 @@
                 kv_quad_got(hh, sel, 2).wait_recv()
                 kv_quad_got(hh, sel, 3).wait_recv()
         for way in range(2):
-            go(ring(hh, way, 0, half))
+            go_ring(hh, way, 0, half)
 
     def pump(hh, distance):
         for half in range(2):
             for way in range(2):
-                if distance <= reach(hh, way):
-                    ring_got(hh, way, distance, half).wait_recv()
-                    if distance < reach(hh, way):
-                        go(ring(hh, way, distance, half))
+                if distance <= reach(way, half):
+                    @pl.when(comes(way, distance, half))
+                    def _():
+                        ring_got(hh, way, distance, half).wait_recv()
+
+                    if distance < reach(way, half):
+                        go_ring(hh, way, distance, half)
 
     def column(h):
         lanes = lax.broadcasted_iota(jnp.int32, (DH, LHEADS), 1)
@@ -336,15 +366,14 @@
             over_heads(lambda j: attend(hh, 1, j, slot, False, False))
 
     def process(hh, distance):
-        ways = [way for way in range(2) if distance <= reach(hh, way)]
-        if len(ways) == 2:
+        if distance < 4:
             def step(way, carry):
                 other_slot(hh, (z + NZ - distance + 2 * distance * way) % NZ)
                 return carry
 
             lax.fori_loop(0, 2, step, 0)
         else:
-            other_slot(hh, (z + (NZ - distance if ways[0] == 0 else distance)) % NZ)
+            other_slot(hh, (z + distance) % NZ)
 
     def finish_heads(hh):
         for half in range(2):
@@ -520,9 +549,9 @@
     pump(0, 2)
     pump(1, 2)
     owner_1()
-    enter_send(0)
     process(0, 2)
     pump(0, 3)
+    enter_send(0)
     process(1, 2)
     pump(1, 3)
     enter_send(1)
@@ -566,6 +595,28 @@
 
     for copy in sends:
         copy.wait_send()
+    for hh, way, step, half in ring_sends:
+        @pl.when(goes(way, step, half))
+        def _():
+            ring(hh, way, step, half).wait_send()
+
+
+def hand_over(light_in, state_in, attn_in, light_out, state_out, attn_out, light, state, attn, sem):
+    rows = light.shape[0] // 4
+    moves = [(state_in, state, state_out)]
+    for i in range(4):
+        part = pl.ds(i * rows, rows)
+        moves.append((light_in.at[part, :], light.at[part, :], light_out.at[part, :]))
+        moves.append((attn_in.at[part, :], attn.at[part, :], attn_out.at[part, :]))
+    into = [pltpu.make_async_copy(a, b, sem.at[0, i]) for i, (a, b, _) in enumerate(moves)]
+    out = [pltpu.make_async_copy(b, a, sem.at[1, i]) for i, (_, b, a) in enumerate(moves)]
+    for copy in into:
+        copy.start()
+    for i in range(len(moves)):
+        into[i].wait()
+        out[i].start()
+    for copy in out:
+        copy.wait()
 
 
 def shards(*arrays):
@@ -576,14 +627,15 @@
     vmem = pl.BlockSpec(memory_space=pltpu.VMEM)
     dma = pltpu.SemaphoreType.DMA
     state = (DH, DH)
-    return pl.pallas_call(
+    shapes = (
+        jax.ShapeDtypeStruct((rows, width), BF16),
+        jax.ShapeDtypeStruct(state_in.shape, F32),
+        jax.ShapeDtypeStruct((rows, width), BF16),
+    )
+    results = pl.pallas_call(
         kernel,
-        out_shape=(
-            jax.ShapeDtypeStruct((rows, width), BF16),
-            jax.ShapeDtypeStruct(state_in.shape, F32),
-            jax.ShapeDtypeStruct((rows, width), BF16),
-        ),
-        in_specs=[hbm, hbm, hbm, vmem, hbm, vmem, hbm, hbm, hbm, hbm],
+        out_shape=shapes,
+        in_specs=[hbm, hbm, hbm, hbm, hbm, vmem, hbm, hbm, hbm, hbm],
         out_specs=(hbm, hbm, hbm),
         scratch_shapes=[
             pltpu.VMEM((NZ, 2, 2, 2, 2 * DH, DH), BF16),
@@ -617,7 +669,8 @@
             pltpu.VMEM((2, LHEADS, DH), F32),
             pltpu.VMEM((NZ, LHEADS, DH), F32),
             pltpu.VMEM(state, F32),
-            dma((5,)),
+            pltpu.VMEM((LHEADS, rows), BF16),
+            dma((6,)),
             dma((2, 2, 4)), dma((2, 2, 4)),
             dma((2, 4)), dma((2, 4)),
             dma, dma((2,)),
@@ -638,9 +691,23 @@
         ),
         name="window",
     )(
-        query_lin, key_lin, value_lin, log_decay, out_gate, norm_gain.reshape(1, width), state_in,
+        query_lin, key_lin, value_lin, log_decay.T, out_gate, norm_gain.reshape(1, width), state_in,
         query_soft, key_soft, value_soft,
     )
+    return pl.pallas_call(
+        hand_over,
+        out_shape=shapes,
+        in_specs=[hbm, hbm, hbm],
+        out_specs=(hbm, hbm, hbm),
+        scratch_shapes=[
+            pltpu.VMEM((rows, width), BF16),
+            pltpu.VMEM(state_in.shape, F32),
+            pltpu.VMEM((rows, width), BF16),
+            dma((2, 9)),
+        ],
+        compiler_params=pltpu.CompilerParams(vmem_limit_bytes=62 * 2**20),
+        name="hand_over",
+    )(*results)
 
 
 def solution(mesh):

time: 94.7 us -> 89.1 us (0.941)
  the two profiles are of different devices: /device:TPU:1 before, /device:TPU:241 now
where the time goes in v3:
time: 89.1 us; the launch traced here: 88.8 us
  Pallas kernels  88 us (99%)
    pallas_call x1, Pallas kernels, shards(): pl.pallas_call(kernel, out_shape=shapes, in_specs=[hbm, hbm, hbm, hbm, hb...  85.5 us
    pallas_call x1, Pallas kernels, shards(): pl.pallas_call(hand_over, out_shape=shapes, in_specs=[hbm, hbm, hbm], out...  2.45 us

profile of v3, /device:TPU:241, one launch (start us, length us, event | category | flops | bytes accessed | tf_op | source)
XLA Modules:
  0.0 88.8 jit_solution(14596751755223399887)
XLA Ops:
  0.6 85.5 %window.1 = (bf16[128,4096]{1,0:T(8,128)(2,1)}, f32[1,128,128]{2,1,0:T(8,128)}, bf16[128,4096]{1,0:T(8,128)(2,1)}) custom-call(bf16[128,4096]{1,0:T(8,128)(2,1)} %ql_in.1, bf16[128,4096]{1,0:T(8,128)(2,1)} %kl_in.1, bf16[128,4096]{1,0:T(8,128)(2,1)} %vl_in.1, bf16[32,128]{1,0:T(8,128)(2,1)} %bitcast.3, bf16[128,4096]{1,0:T(8,128)(2,1)} %gate_in.1, ...), custom_call_target="tpu_custom_call" | custom-call | tf_op jit(solution)/shard_map/window/pallas_call | solution.py:635
  86.2 2.5 %hand_over.1 = (bf16[128,4096]{1,0:T(8,128)(2,1)}, f32[1,128,128]{2,1,0:T(8,128)}, bf16[128,4096]{1,0:T(8,128)(2,1)}) custom-call(bf16[128,4096]{1,0:T(8,128)(2,1)} %get-tuple-element.6.light_in, f32[1,128,128]{2,1,0:T(8,128)} %get-tuple-element.7.state_in, bf16[128,4096]{1,0:T(8,128)(2,1)} %get-tuple-element.8.attn_in), custom_call_target="tpu_custom_call" | custom-call | tf_op jit(solution)/shard_map/hand_over/pallas_call | solution.py:697

commit v4 on v3

--- a/solution.py
+++ b/solution.py
@@ -271,7 +271,7 @@
     remote(dt.at[c], dt.at[1 - c], d_s, d_r, mate_at(1)).wait_recv()
     remote(s_oth, s_par, sp_s, sp_r, mate_at(1)).wait_recv()
     first = c == 0
-    chd[z] = dt[0] + dt[1]
+    chd[z] = jnp.transpose(dt[0] + dt[1])[0:8, :]
 
     def chip_state(n, carry):
         h = head_of(n, c)
@@ -311,24 +311,27 @@
         heads = pl.ds(pl.multiple_of(j * DH, DH), DH)
         queries = jnp.concatenate([qx[hh, 2 * half, :, heads], qx[hh, 2 * half + 1, :, heads]], axis=0)
         parts = (0, 1) if both else (0,)
-        keys = jnp.concatenate([kv[slot, hh, i, 0] for i in parts], axis=0)
-        values = jnp.concatenate(
-            [kv[slot, hh, i, 1, b * DH : (b + 1) * DH, :] for i in parts for b in range(2)], axis=1
-        )
-        s = lax.dot_general(keys, queries, ROWS_BY_ROWS, preferred_element_type=F32)
+        row = pl.ds(half * 4 + j, 1)
+        scores = [
+            lax.dot_general(kv[slot, hh, i, 0], queries, ROWS_BY_ROWS, preferred_element_type=F32)
+            for i in parts
+        ]
         if own:
-            count = s.shape[0]
-            key = lax.broadcasted_iota(jnp.int32, s.shape, 0) - (count - 2 * DH)
-            query = lax.broadcasted_iota(jnp.int32, s.shape, 1)
-            s = jnp.where(key <= query, s, MASKED)
-        row = pl.ds(half * 4 + j, 1)
-        new = jnp.max(s, axis=0, keepdims=True)
+            key = lax.broadcasted_iota(jnp.int32, (2 * DH, 2 * DH), 0)
+            query = lax.broadcasted_iota(jnp.int32, (2 * DH, 2 * DH), 1)
+            scores[-1] = jnp.where(key <= query, scores[-1], MASKED)
+        new = functools.reduce(jnp.maximum, [jnp.max(s, axis=0, keepdims=True) for s in scores])
         if not own:
             old = top[hh, row, :]
             new = jnp.maximum(old, new)
-        raised = jnp.exp2((s - new) * EXP2_SCALE)
-        part = jnp.sum(raised, axis=0, keepdims=True)
-        summed = jnp.dot(values, raised.astype(BF16), preferred_element_type=F32)
+        part, summed = None, None
+        for i, s in zip(parts, scores):
+            raised = jnp.exp2((s - new) * EXP2_SCALE)
+            values = jnp.concatenate([kv[slot, hh, i, 1, :DH, :], kv[slot, hh, i, 1, DH:, :]], axis=1)
+            more = jnp.sum(raised, axis=0, keepdims=True)
+            product = jnp.dot(values, raised.astype(BF16), preferred_element_type=F32)
+            part = more if part is None else part + more
+            summed = product if summed is None else summed + product
         if own:
             low[hh, row, :] = part
             acc[hh, half, j] = summed
@@ -443,11 +446,13 @@
         )
 
     def prefix():
+        lanes = lax.broadcasted_iota(jnp.int32, (8, LHEADS), 1)
         for k in range(2):
             state = fin[k]
             for zi in range(NZ):
                 eout[zi, k] = state.astype(BF16)
-                decay = jnp.exp(chd[zi, pl.ds(16 * k + 2 * z + c, 1), :])
+                total = jnp.where(lanes == 16 * k + 2 * z + c, chd[zi], 0.0)
+                decay = jnp.exp(jnp.sum(total, axis=1, keepdims=True))[0:1, :]
                 state = decay * state + sgot[zi, k].astype(F32)
             fin[k] = state
 
@@ -538,26 +543,26 @@
     pump(0, 1)
     inner_heads(16, 32)
     pump(1, 1)
+    loads[4].wait()
+    gates()
     queries_here(0)
     own_slot(0)
     process(0, 1)
     queries_here(1)
+    pump(0, 2)
     own_slot(1)
     states_here()
     owner_0()
+    pump(1, 2)
     process(1, 1)
-    pump(0, 2)
-    pump(1, 2)
     owner_1()
-    process(0, 2)
     pump(0, 3)
     enter_send(0)
+    process(0, 2)
     process(1, 2)
     pump(1, 3)
     enter_send(1)
     process(0, 3)
-    loads[4].wait()
-    gates()
     pump(0, 4)
     process(0, 4)
     finish_heads(0)
@@ -667,7 +672,7 @@
             pltpu.VMEM((2,) + state, F32),
             pltpu.VMEM((2,) + state, F32),
             pltpu.VMEM((2, LHEADS, DH), F32),
-            pltpu.VMEM((NZ, LHEADS, DH), F32),
+            pltpu.VMEM((NZ, 8, LHEADS), F32),
             pltpu.VMEM(state, F32),
             pltpu.VMEM((LHEADS, rows), BF16),
             dma((6,)),

time: 89.1 us -> 85.1 us (0.955)
  the two profiles are of different devices: /device:TPU:241 before, /device:TPU:1 now
where the time goes in v4:
time: 85.1 us; the launch traced here: 83.4 us
  Pallas kernels  82.6 us (97%)
    pallas_call x1, Pallas kernels, shards(): pl.pallas_call(kernel, out_shape=shapes, in_specs=[hbm, hbm, hbm, hbm, hb...  80.1 us
    pallas_call x1, Pallas kernels, shards(): pl.pallas_call(hand_over, out_shape=shapes, in_specs=[hbm, hbm, hbm], out...  2.45 us

profile of v4, /device:TPU:1, one launch (start us, length us, event | category | flops | bytes accessed | tf_op | source)
XLA Modules:
  0.0 83.4 jit_solution(6494775989201504092)
XLA Ops:
  0.6 80.1 %window.1 = (bf16[128,4096]{1,0:T(8,128)(2,1)}, f32[1,128,128]{2,1,0:T(8,128)}, bf16[128,4096]{1,0:T(8,128)(2,1)}) custom-call(bf16[128,4096]{1,0:T(8,128)(2,1)} %ql_in.1, bf16[128,4096]{1,0:T(8,128)(2,1)} %kl_in.1, bf16[128,4096]{1,0:T(8,128)(2,1)} %vl_in.1, bf16[32,128]{1,0:T(8,128)(2,1)} %bitcast.3, bf16[128,4096]{1,0:T(8,128)(2,1)} %gate_in.1, ...), custom_call_target="tpu_custom_call" | custom-call | tf_op jit(solution)/shard_map/window/pallas_call | solution.py:640
  80.8 2.5 %hand_over.1 = (bf16[128,4096]{1,0:T(8,128)(2,1)}, f32[1,128,128]{2,1,0:T(8,128)}, bf16[128,4096]{1,0:T(8,128)(2,1)}) custom-call(bf16[128,4096]{1,0:T(8,128)(2,1)} %get-tuple-element.6.light_in, f32[1,128,128]{2,1,0:T(8,128)} %get-tuple-element.7.state_in, bf16[128,4096]{1,0:T(8,128)(2,1)} %get-tuple-element.8.attn_in), custom_call_target="tpu_custom_call" | custom-call | tf_op jit(solution)/shard_map/hand_over/pallas_call | solution.py:702

commit v5 on v4

--- a/solution.py
+++ b/solution.py
@@ -223,7 +223,7 @@
             target[n] = state.astype(target.dtype)
             return carry
 
-        lax.fori_loop(0, 16, step, 0, unroll=4)
+        lax.fori_loop(0, 16, step, 0, unroll=8)
 
     start_ring(0, 0)
     start_ring(1, 0)
@@ -379,7 +379,7 @@
             other_slot(hh, (z + distance) % NZ)
 
     def finish_heads(hh):
-        for half in range(2):
+        for half, mates_now in ((1 - x, (2, 3)), (x, (1,))):
             def step(j, carry):
                 scale = 1.0 / low[hh, pl.ds(half * 4 + j, 1), :]
                 result = jnp.transpose(acc[hh, half, j] * scale).astype(BF16)
@@ -388,8 +388,8 @@
                 return carry
 
             lax.fori_loop(0, 4, step, 0, unroll=2)
-        for p in (2, 3, 1):
-            go(out_quad(hh, p))
+            for p in mates_now:
+                go(out_quad(hh, p))
         out_own(hh).start()
 
     def out_quad(hh, p):
@@ -427,7 +427,7 @@
             lin[:, block(h)] = jnp.dot(damped, vlv[:, block(h)], preferred_element_type=F32)
             return carry
 
-        lax.fori_loop(begin, end, step, 0, unroll=4)
+        lax.fori_loop(begin, end, step, 0, unroll=8)
 
     t_move = remote(fin, t0, t_s, t_r, mate_at(2))
     so_move = remote(fin.at[0], state_out.at[0], so_s, so_r.at[0], mate_at(2))
@@ -567,12 +567,12 @@
     process(0, 4)
     finish_heads(0)
     process(1, 3)
+    pump(1, 4)
+    process(1, 4)
+    finish_heads(1)
     pair_enter(0)
     sq[...] = jnp.zeros_like(sq)
     carried(c, 0)
-    pump(1, 4)
-    process(1, 4)
-    finish_heads(1)
     enter_pair_got(0).wait_recv()
     carried(1 - c, 0)
     pair_enter(1)

time: 85.1 us -> 84.2 us (0.989); the launches traced: 83.4 us -> 83.4 us
  no operation moved by 1% of the time
where the time goes in v5:
time: 84.2 us; the launch traced here: 83.4 us
  Pallas kernels  82.5 us (98%)
    pallas_call x1, Pallas kernels, shards(): pl.pallas_call(kernel, out_shape=shapes, in_specs=[hbm, hbm, hbm, hbm, hb...  80.1 us
    pallas_call x1, Pallas kernels, shards(): pl.pallas_call(hand_over, out_shape=shapes, in_specs=[hbm, hbm, hbm], out...  2.45 us

profile of v5, /device:TPU:1, one launch (start us, length us, event | category | flops | bytes accessed | tf_op | source)
XLA Modules:
  0.0 83.4 jit_solution(17602683009520498284)
XLA Ops:
  0.6 80.1 %window.1 = (bf16[128,4096]{1,0:T(8,128)(2,1)}, f32[1,128,128]{2,1,0:T(8,128)}, bf16[128,4096]{1,0:T(8,128)(2,1)}) custom-call(bf16[128,4096]{1,0:T(8,128)(2,1)} %ql_in.1, bf16[128,4096]{1,0:T(8,128)(2,1)} %kl_in.1, bf16[128,4096]{1,0:T(8,128)(2,1)} %vl_in.1, bf16[32,128]{1,0:T(8,128)(2,1)} %bitcast.3, bf16[128,4096]{1,0:T(8,128)(2,1)} %gate_in.1, ...), custom_call_target="tpu_custom_call" | custom-call | tf_op jit(solution)/shard_map/window/pallas_call | solution.py:640
  80.7 2.5 %hand_over.1 = (bf16[128,4096]{1,0:T(8,128)(2,1)}, f32[1,128,128]{2,1,0:T(8,128)}, bf16[128,4096]{1,0:T(8,128)(2,1)}) custom-call(bf16[128,4096]{1,0:T(8,128)(2,1)} %get-tuple-element.6.light_in, f32[1,128,128]{2,1,0:T(8,128)} %get-tuple-element.7.state_in, bf16[128,4096]{1,0:T(8,128)(2,1)} %get-tuple-element.8.attn_in), custom_call_target="tpu_custom_call" | custom-call | tf_op jit(solution)/shard_map/hand_over/pallas_call | solution.py:702

commit v6 on v5

--- a/solution.py
+++ b/solution.py
@@ -283,7 +283,7 @@
         s_own[n] = earlier_state
         return carry
 
-    lax.fori_loop(0, 16, chip_state, 0, unroll=2)
+    lax.fori_loop(0, 16, chip_state, 0, unroll=4)
     sgot[z] = ssend[z]
 
     def chip_decay(k):
@@ -387,7 +387,7 @@
                 ob[hh, 2 * half + 1, :, block(j)] = result[DH:]
                 return carry
 
-            lax.fori_loop(0, 4, step, 0, unroll=2)
+            lax.fori_loop(0, 4, step, 0, unroll=4)
             for p in mates_now:
                 go(out_quad(hh, p))
         out_own(hh).start()
@@ -497,7 +497,7 @@
             esend[part, zi] = jnp.where(first, after, entering)
             return carry
 
-        lax.fori_loop(0, NZ, step, 0, unroll=2)
+        lax.fori_loop(0, NZ, step, 0, unroll=4)
         go(enter_pair(part))
 
     def enter_pair(part):
@@ -515,7 +515,7 @@
             sq[...] += mixed * mixed
             return carry
 
-        lax.fori_loop(0, NZ, step, 0, unroll=4)
+        lax.fori_loop(0, NZ, step, 0, unroll=8)
 
     def gates():
         def step(h, carry):
@@ -533,7 +533,7 @@
             qlv[:, block(h)] = (lin[:, block(h)] * factor * gf[:, block(h)]).astype(BF16)
             return carry
 
-        lax.fori_loop(0, LHEADS, gated, 0, unroll=4)
+        lax.fori_loop(0, LHEADS, gated, 0, unroll=8)
         light_copy.start()
 
     light_copy = pltpu.make_async_copy(qlv, light_out, out_s)

time: 84.2 us -> 84.1 us (level)
  no operation moved by 1% of the time
where the time goes in v6:
time: 84.1 us; the launch traced here: 83.2 us
  Pallas kernels  82.4 us (98%)
    pallas_call x1, Pallas kernels, shards(): pl.pallas_call(kernel, out_shape=shapes, in_specs=[hbm, hbm, hbm, hbm, hb...  80 us
    pallas_call x1, Pallas kernels, shards(): pl.pallas_call(hand_over, out_shape=shapes, in_specs=[hbm, hbm, hbm], out...  2.45 us

profile of v6, /device:TPU:1, one launch (start us, length us, event | category | flops | bytes accessed | tf_op | source)
XLA Modules:
  0.0 83.2 jit_solution(13822901171899890954)
XLA Ops:
  0.6 80.0 %window.1 = (bf16[128,4096]{1,0:T(8,128)(2,1)}, f32[1,128,128]{2,1,0:T(8,128)}, bf16[128,4096]{1,0:T(8,128)(2,1)}) custom-call(bf16[128,4096]{1,0:T(8,128)(2,1)} %ql_in.1, bf16[128,4096]{1,0:T(8,128)(2,1)} %kl_in.1, bf16[128,4096]{1,0:T(8,128)(2,1)} %vl_in.1, bf16[32,128]{1,0:T(8,128)(2,1)} %bitcast.3, bf16[128,4096]{1,0:T(8,128)(2,1)} %gate_in.1, ...), custom_call_target="tpu_custom_call" | custom-call | tf_op jit(solution)/shard_map/window/pallas_call | solution.py:640
  80.6 2.5 %hand_over.1 = (bf16[128,4096]{1,0:T(8,128)(2,1)}, f32[1,128,128]{2,1,0:T(8,128)}, bf16[128,4096]{1,0:T(8,128)(2,1)}) custom-call(bf16[128,4096]{1,0:T(8,128)(2,1)} %get-tuple-element.6.light_in, f32[1,128,128]{2,1,0:T(8,128)} %get-tuple-element.7.state_in, bf16[128,4096]{1,0:T(8,128)(2,1)} %get-tuple-element.8.attn_in), custom_call_target="tpu_custom_call" | custom-call | tf_op jit(solution)/shard_map/hand_over/pallas_call | solution.py:702
